TPU v7x, 512 devices: a whole 4x4x16 slice. The times are simulated.
512 devices in a mesh: row: 32 (over z, core), col: 16 (over x, y).
Axes of the slice: x: 4, y: 4, z: 16, core: 2. Of those that a mesh axis runs over, the one named last changes fastest.
Arguments:
- boxes: int32 [4, 2097152], P(None, ('row', 'col')), may hold values from 0 to 4095, as said below
- pins: int32 [2097152], P(('row', 'col')), may hold values from 2 to 32
- cell_bins: int32 [2, 8388608], P(None, ('row', 'col')), may hold values from 0 to 4095, as said below
- cell_area: int32 [8388608], P(('row', 'col')), may hold values from 1 to 64
Outputs:
- demand: float32 [4096, 4096], P('row', 'col')
- density: float32 [4096, 4096], P('row', 'col')
Inputs may be any that keep to these rules, and one draw needn't show every extreme that they name: `boxes`: nets are in blocks of 4096, one block per device in the order of the row+col index; the lower corner (y0, x0) of a net lies in that device's 128 x 256 bins. y0 <= y1 < 4096, x0 <= x1 < 4096, y1 - y0 + 1 <= 64 and x1 - x0 + 1 <= 128. `cell_bins`: cells are in blocks of 16384, one block per device in the order of the row+col index; each cell's bin lies in that device's bins.
All inputs are finite; a program needn't handle non-finite values.
Results may differ from a plain program's by a relative error of at most 0.0025.
Values sent between devices are 32-bit elements; how exact they have to be, the bound alone decides.
No kernel may reach another device: no remote copies, remote signals or barrier semaphores. Data moves between devices by JAX's collectives and lax.ppermute only.
A program may use at most 64 MiB of HBM per device.

v0:
```python
import math

import jax
import jax.numpy as jnp
from jax import lax
from jax.sharding import PartitionSpec as P

BR = 128
BC = 256
STEPS = 6


def from_behind(block, axis, distance):
    devices = range(lax.axis_size(axis))
    route = [(i - distance, i) for i in devices if i - distance in devices]
    return lax.ppermute(block, axis, route)


def entering(value, axis, combine, identity):
    length, here = (lax.axis_size(axis), lax.axis_index(axis))
    everything = lax.all_gather(value, axis)
    start = jnp.broadcast_to(jnp.asarray(identity, value.dtype), value.shape)

    def step(k, before):
        reached = k < here
        new = combine(before, everything[k])
        return jnp.where(reached, new, before)

    return lax.fori_loop(0, length, step, start)


def padded_2(block, sides, width):
    for axis, dim in sides:
        count = lax.axis_size(axis)
        forward = [(i, i + 1) for i in range(count - 1)]
        backward = [(target, source) for source, target in forward]
        low = lax.ppermute(
            lax.slice_in_dim(block, block.shape[dim] - width, None, axis=dim), axis, forward
        )
        high = lax.ppermute(lax.slice_in_dim(block, 0, width, axis=dim), axis, backward)
        block = jnp.concatenate([low, block, high], axis=dim)
    return block


def impulse_tile(boxes, pins, row_first, col_first, nrows, ncols):
    count = pins.shape[0]
    block = math.gcd(count, 256)
    groups = count // block
    box_blocks = jnp.transpose(boxes.reshape(4, groups, block), (1, 0, 2))
    pin_blocks = pins.reshape(groups, block)

    def impulse_add_block(tile, item):
        box, pin = item
        width = (box[3] - box[2] + 1).astype(jnp.float32)
        height = (box[1] - box[0] + 1).astype(jnp.float32)
        weight = pin.astype(jnp.float32) * (width + height) / (width * height) / 16.0
        weight_high = weight.astype(jnp.bfloat16)
        rest = weight - weight_high.astype(jnp.float32)
        weight_mid = rest.astype(jnp.bfloat16)
        weight_low = (rest - weight_mid.astype(jnp.float32)).astype(jnp.bfloat16)
        rows = lax.broadcasted_iota(jnp.int32, (nrows, block), 0) + row_first
        left = (
            (rows == box[0][None, :]).astype(jnp.int32)
            - (rows == box[1][None, :] + 1).astype(jnp.int32)
        ).astype(jnp.bfloat16)
        cols = lax.broadcasted_iota(jnp.int32, (block, ncols), 1) + col_first
        signs = (
            (cols == box[2][:, None]).astype(jnp.int32)
            - (cols == box[3][:, None] + 1).astype(jnp.int32)
        ).astype(jnp.bfloat16)
        left_three = jnp.concatenate([left, left, left], axis=1)
        right_three = jnp.concatenate(
            [
                signs * weight_high[:, None],
                signs * weight_mid[:, None],
                signs * weight_low[:, None],
            ],
            axis=0,
        )
        return (tile + jnp.dot(left_three, right_three, preferred_element_type=jnp.float32), None)

    start = jnp.zeros((nrows, ncols), jnp.float32)
    tile, unused = lax.scan(impulse_add_block, start, (box_blocks, pin_blocks))
    return tile


def area_tile(cell_bins, cell_area, row_first, col_first):
    count = cell_area.shape[0]
    block = math.gcd(count, 512)
    groups = count // block
    bin_blocks = jnp.transpose(cell_bins.reshape(2, groups, block), (1, 0, 2))
    area_blocks = cell_area.reshape(groups, block)

    def area_add_block(tile, item):
        where, area = item
        rows = lax.broadcasted_iota(jnp.int32, (BR, block), 0) + row_first
        left = (rows == where[0][None, :]).astype(jnp.bfloat16)
        cols = lax.broadcasted_iota(jnp.int32, (block, BC), 1) + col_first
        right = jnp.where(cols == where[1][:, None], area.astype(jnp.float32)[:, None], 0.0).astype(
            jnp.bfloat16
        )
        return (tile + jnp.dot(left, right, preferred_element_type=jnp.float32), None)

    tile, unused = lax.scan(
        area_add_block, jnp.zeros((BR, BC), jnp.float32), (bin_blocks, area_blocks)
    )
    return tile


def diffuse(padded):
    middle = padded[1:-1, 1:-1]
    beside = padded[2:, 1:-1] + padded[:-2, 1:-1] + padded[1:-1, 2:] + padded[1:-1, :-2]
    return middle + 0.24 * (beside - 4.0 * middle)


def body(boxes, pins, cell_bins, cell_area):
    row_pos = lax.axis_index("row")
    col_pos = lax.axis_index("col")
    row_first = row_pos * BR
    col_first = col_pos * BC
    wide = impulse_tile(boxes, pins, row_first, col_first, 2 * BR, 2 * BC)
    from_left, from_corner = from_behind((wide[:BR, BC:], wide[BR:, BC:]), "col", 1)
    from_above = from_behind(wide[BR:, :BC] + from_corner, "row", 1)
    impulse = wide[:BR, :BC] + from_left + from_above
    upper = (
        lax.broadcasted_iota(jnp.int32, (BC, BC), 0) <= lax.broadcasted_iota(jnp.int32, (BC, BC), 1)
    ).astype(jnp.float32)
    across = jnp.dot(
        impulse, upper, precision=lax.Precision.HIGHEST, preferred_element_type=jnp.float32
    )
    row_carry = entering(
        across[:, -1], "col", lambda earlier, later: earlier + later, jnp.zeros((BR,), jnp.float32)
    )
    across = across + row_carry[:, None]
    lower = (
        lax.broadcasted_iota(jnp.int32, (BR, BR), 0) >= lax.broadcasted_iota(jnp.int32, (BR, BR), 1)
    ).astype(jnp.float32)
    downward = jnp.dot(
        lower, across, precision=lax.Precision.HIGHEST, preferred_element_type=jnp.float32
    )
    col_carry = entering(
        downward[-1, :],
        "row",
        lambda earlier, later: earlier + later,
        jnp.zeros((BC,), jnp.float32),
    )
    demand = downward + col_carry[None, :]
    area_sum = area_tile(cell_bins, cell_area, row_first, col_first)
    density = (1.0 + 1.5 * demand / (1.0 + demand)) * area_sum / 16.0
    for step in range(STEPS):
        padded = padded_2(density, (("row", 0), ("col", 1)), 1)
        density = diffuse(padded)
    return (demand, density)


def solution(mesh):
    return jax.shard_map(
        body,
        mesh=mesh,
        in_specs=(
            P(None, ("row", "col")),
            P(("row", "col")),
            P(None, ("row", "col")),
            P(("row", "col")),
        ),
        out_specs=(P("row", "col"), P("row", "col")),
        check_vma=False,
    )
```

profile of v0, /device:TPU:130, one launch (start us, length us, event | category | flops | bytes accessed | tf_op | source)
XLA Modules:
  0.0 257.6 jit_solution(2748684562905251650)
XLA Ops:
  1.4 28.4 %while.50 = (s32[]{:T(128)}, f32[256,512]{1,0:T(8,128)S(1)}, s32[]{:T(128)}, s32[16,4,256]{2,1,0:T(4,128)}, s32[]{:T(128)}, /*index=5*/s32[16,256]{1,0:T(8,128)S...) while((s32[]{:T(128)}, f32[256,512]{1,0:T(8,128)S(1)}, s32[]{:T(128)}, ...), condition=%wide.region_1.2_spmd.clone, body=%wide.region_0.1_spmd.clone.sunk | while | flops 206706944 | bytes 2918583 | solution.py:83
  4.9 0.8 constant_dynamic-slice_fusion.11
  6.7 0.8 constant_dynamic-slice_fusion.11
  8.5 0.8 constant_dynamic-slice_fusion.11
  29.8 3.5 %collective-permute-start.1 = (f32[128,256]{1,0:T(8,128)S(1)}, f32[128,256]{1,0:T(8,128)S(1)}, u32[]{:S(2)}, u32[]{:S(2)}) collective-permute-start(f32[128,256]{1,0:T(8,128)S(1)} %get-tuple-element.358), channel_id=1, source_target_pairs={{0,1},{1,2},{2,3},{3,4},{4,5},{5,6},{6,7},{7,8},{8,9},{9,10},{10,1... | collective-permute-start | bytes 393224 | tf_op jit(solution)/shard_map/ppermute | solution.py:16
  33.3 3.5 %collective-permute-start = (f32[128,256]{1,0:T(8,128)S(1)}, f32[128,256]{1,0:T(8,128)S(1)}, u32[]{:S(2)}, u32[]{:S(2)}) collective-permute-start(f32[128,256]{1,0:T(8,128)S(1)} %get-tuple-element.357), channel_id=1, source_target_pairs={{0,1},{1,2},{2,3},{3,4},{4,5},{5,6},{6,7},{7,8},{8,9},{9,10},{10,1... | collective-permute-start | bytes 393224 | tf_op jit(solution)/shard_map/ppermute | solution.py:16
  36.8 2.2 collective-permute-done.1
  39.0 1.9 collective-permute-start.2
  41.0 39.2 %while.53 = (s32[]{:T(128)}, f32[128,256]{1,0:T(8,128)S(1)}, s32[]{:T(128)}, s32[32,2,512]{2,1,0:T(2,128)}, s32[]{:T(128)}, /*index=5*/s32[32,512]{1,0:T(8,128)S(1)}, s32[]{:T(128)}, s32[]{:T(128)}, s32[]{}) while((s32[]{:T(128)}, f32[128,256]{1,0:T(8,128)S(1)}, s32[]{:T(128)}, s32[32,2,512]{2,1,0:T(2,128)}, s32[]{:T(128)}, ...), condition=%wide.region_7.8_spmd.clone, body=%wide.region_6.7_spmd.clone.sunk | while | flops 33948548 | bytes 283783 | solution.py:104
  80.5 24.0 %all-gather = f32[2048,1]{1,0:T(8,128)S(1)} all-gather(f32[128,1]{1,0:T(8,128)S(1)} %slice.277), channel_id=2, replica_groups=mesh['row'=32,'col'=16] {'col'}, dimensions={0}, use_global_device_ids=true | all-gather | bytes 8704 | tf_op jit(solution)/shard_map/all_gather | solution.py:21
  105.9 30.2 %all-gather.1 = f32[32,1,256]{2,1,0:T(1,128)S(1)} all-gather(f32[1,1,256]{2,1,0:T(1,128)S(1)} %slice_bitcast_fusion), channel_id=1, replica_groups=mesh['row'=32,'col'=16] {'row'}, dimensions={0}, use_global_device_ids=true | all-gather | bytes 33792 | tf_op jit(solution)/shard_map/all_gather | solution.py:21
  136.2 1.7 while.52
  137.9 2.9 %collective-permute-start.3 = (f32[1,256]{1,0:T(1,128)S(1)}, f32[1,256]{1,0:T(1,128)S(1)}, u32[]{:S(2)}, u32[]{:S(2)}) collective-permute-start(f32[1,256]{1,0:T(1,128)S(1)} %get-tuple-element.382), channel_id=1, source_target_pairs={{16,0},{32,16},{48,32},{64,48},{80,64},{96,80},{112,96},{128,112},... | collective-permute-start | bytes 3080 | tf_op jit(solution)/shard_map/ppermute | solution.py:40
  140.8 1.9 collective-permute-start.4
  142.8 4.2 %collective-permute-done.4 = f32[1,256]{1,0:T(1,128)S(1)} collective-permute-done((f32[1,256]{1,0:T(1,128)S(1)}, f32[1,256]{1,0:T(1,128)S(1)}, u32[]{:S(2)}, u32[]{:S(2)}) %collective-permute-start.4) | collective-permute-done | bytes 1056 | tf_op jit(solution)/shard_map/ppermute | solution.py:37
  147.0 4.6 %collective-permute-start.5 = (f32[130,1]{1,0:T(8,128)S(1)}, f32[130,1]{1,0:T(8,128)S(1)}, u32[]{:S(2)}, u32[]{:S(2)}) collective-permute-start(f32[130,1]{1,0:T(8,128)S(1)} %get-tuple-element.369), channel_id=1, source_target_pairs={{1,0},{2,1},{3,2},{4,3},{5,4},{6,5},{7,6},{8,7},{9,8},{10,9},{11,1... | collective-permute-start | bytes 1568 | tf_op jit(solution)/shard_map/ppermute | solution.py:40
  151.6 1.9 collective-permute-start.6
  153.5 6.4 %collective-permute-done.6 = f32[130,1]{1,0:T(8,128)S(1)} collective-permute-done((f32[130,1]{1,0:T(8,128)S(1)}, f32[130,1]{1,0:T(8,128)S(1)}, u32[]{:S(2)}, u32[]{:S(2)}) %collective-permute-start.6) | collective-permute-done | bytes 552 | tf_op jit(solution)/shard_map/ppermute | solution.py:37
  160.1 1.9 collective-permute-start.7
  162.0 2.4 collective-permute-start.8
  164.4 3.7 %collective-permute-done.8 = f32[1,256]{1,0:T(1,128)S(1)} collective-permute-done((f32[1,256]{1,0:T(1,128)S(1)}, f32[1,256]{1,0:T(1,128)S(1)}, u32[]{:S(2)}, u32[]{:S(2)}) %collective-permute-start.8) | collective-permute-done | bytes 1056 | tf_op jit(solution)/shard_map/ppermute | solution.py:37
  168.2 1.9 collective-permute-start.10
  170.1 6.0 %collective-permute-start.9 = (f32[130,1]{1,0:T(8,128)S(1)}, f32[130,1]{1,0:T(8,128)S(1)}, u32[]{:S(2)}, u32[]{:S(2)}) collective-permute-start(f32[130,1]{1,0:T(8,128)S(1)} %get-tuple-element.367), channel_id=1, source_target_pairs={{1,0},{2,1},{3,2},{4,3},{5,4},{6,5},{7,6},{8,7},{9,8},{10,9},{11,1... | collective-permute-start | bytes 1568 | tf_op jit(solution)/shard_map/ppermute | solution.py:40
  176.5 1.6 collective-permute-done.9
  178.3 1.9 collective-permute-start.11
  180.2 2.4 collective-permute-start.12
  182.6 3.7 %collective-permute-done.12 = f32[1,256]{1,0:T(1,128)S(1)} collective-permute-done((f32[1,256]{1,0:T(1,128)S(1)}, f32[1,256]{1,0:T(1,128)S(1)}, u32[]{:S(2)}, u32[]{:S(2)}) %collective-permute-start.12) | collective-permute-done | bytes 1056 | tf_op jit(solution)/shard_map/ppermute | solution.py:37
  186.4 6.4 %collective-permute-start.13 = (f32[130,1]{1,0:T(8,128)S(1)}, f32[130,1]{1,0:T(8,128)S(1)}, u32[]{:S(2)}, u32[]{:S(2)}) collective-permute-start(f32[130,1]{1,0:T(8,128)S(1)} %get-tuple-element.365), channel_id=1, source_target_pairs={{1,0},{2,1},{3,2},{4,3},{5,4},{6,5},{7,6},{8,7},{9,8},{10,9},{11,1... | collective-permute-start | bytes 1568 | tf_op jit(solution)/shard_map/ppermute | solution.py:40
  192.8 1.9 collective-permute-start.14
  194.8 6.4 %collective-permute-done.14 = f32[130,1]{1,0:T(8,128)S(1)} collective-permute-done((f32[130,1]{1,0:T(8,128)S(1)}, f32[130,1]{1,0:T(8,128)S(1)}, u32[]{:S(2)}, u32[]{:S(2)}) %collective-permute-start.14) | collective-permute-done | bytes 552 | tf_op jit(solution)/shard_map/ppermute | solution.py:37
  201.3 1.9 collective-permute-start.15
  203.2 2.4 collective-permute-start.16
  205.7 3.7 %collective-permute-done.16 = f32[1,256]{1,0:T(1,128)S(1)} collective-permute-done((f32[1,256]{1,0:T(1,128)S(1)}, f32[1,256]{1,0:T(1,128)S(1)}, u32[]{:S(2)}, u32[]{:S(2)}) %collective-permute-start.16) | collective-permute-done | bytes 1056 | tf_op jit(solution)/shard_map/ppermute | solution.py:37
  209.4 1.9 collective-permute-start.17
  211.4 3.9 %collective-permute-start.18 = (f32[130,1]{1,0:T(8,128)S(1)}, f32[130,1]{1,0:T(8,128)S(1)}, u32[]{:S(2)}, u32[]{:S(2)}) collective-permute-start(f32[130,1]{1,0:T(8,128)S(1)} %get-tuple-element.364), channel_id=1, source_target_pairs={{0,1},{1,2},{2,3},{3,4},{4,5},{5,6},{6,7},{7,8},{8,9},{9,10},{10,1... | collective-permute-start | bytes 1568 | tf_op jit(solution)/shard_map/ppermute | solution.py:37
  215.6 4.0 %collective-permute-done.18 = f32[130,1]{1,0:T(8,128)S(1)} collective-permute-done((f32[130,1]{1,0:T(8,128)S(1)}, f32[130,1]{1,0:T(8,128)S(1)}, u32[]{:S(2)}, u32[]{:S(2)}) %collective-permute-start.18) | collective-permute-done | bytes 552 | tf_op jit(solution)/shard_map/ppermute | solution.py:37
  219.8 1.9 collective-permute-start.19
  221.8 2.4 collective-permute-start.20
  224.2 3.7 %collective-permute-done.20 = f32[1,256]{1,0:T(1,128)S(1)} collective-permute-done((f32[1,256]{1,0:T(1,128)S(1)}, f32[1,256]{1,0:T(1,128)S(1)}, u32[]{:S(2)}, u32[]{:S(2)}) %collective-permute-start.20) | collective-permute-done | bytes 1056 | tf_op jit(solution)/shard_map/ppermute | solution.py:37
  228.0 1.9 collective-permute-start.21
  229.9 3.9 %collective-permute-start.22 = (f32[130,1]{1,0:T(8,128)S(1)}, f32[130,1]{1,0:T(8,128)S(1)}, u32[]{:S(2)}, u32[]{:S(2)}) collective-permute-start(f32[130,1]{1,0:T(8,128)S(1)} %get-tuple-element.362), channel_id=1, source_target_pairs={{0,1},{1,2},{2,3},{3,4},{4,5},{5,6},{6,7},{7,8},{8,9},{9,10},{10,1... | collective-permute-start | bytes 1568 | tf_op jit(solution)/shard_map/ppermute | solution.py:37
  234.2 4.0 %collective-permute-done.22 = f32[130,1]{1,0:T(8,128)S(1)} collective-permute-done((f32[130,1]{1,0:T(8,128)S(1)}, f32[130,1]{1,0:T(8,128)S(1)}, u32[]{:S(2)}, u32[]{:S(2)}) %collective-permute-start.22) | collective-permute-done | bytes 552 | tf_op jit(solution)/shard_map/ppermute | solution.py:37
  238.4 1.9 collective-permute-start.23
  240.3 2.4 collective-permute-start.24
  242.7 3.7 %collective-permute-done.24 = f32[1,256]{1,0:T(1,128)S(1)} collective-permute-done((f32[1,256]{1,0:T(1,128)S(1)}, f32[1,256]{1,0:T(1,128)S(1)}, u32[]{:S(2)}, u32[]{:S(2)}) %collective-permute-start.24) | collective-permute-done | bytes 1056 | tf_op jit(solution)/shard_map/ppermute | solution.py:37
  246.5 1.9 collective-permute-start.25
  248.4 3.9 %collective-permute-start.26 = (f32[130,1]{1,0:T(8,128)S(1)}, f32[130,1]{1,0:T(8,128)S(1)}, u32[]{:S(2)}, u32[]{:S(2)}) collective-permute-start(f32[130,1]{1,0:T(8,128)S(1)} %get-tuple-element.360), channel_id=1, source_target_pairs={{0,1},{1,2},{2,3},{3,4},{4,5},{5,6},{6,7},{7,8},{8,9},{9,10},{10,1... | collective-permute-start | bytes 1568 | tf_op jit(solution)/shard_map/ppermute | solution.py:37
  252.7 4.0 %collective-permute-done.26 = f32[130,1]{1,0:T(8,128)S(1)} collective-permute-done((f32[130,1]{1,0:T(8,128)S(1)}, f32[130,1]{1,0:T(8,128)S(1)}, u32[]{:S(2)}, u32[]{:S(2)}) %collective-permute-start.26) | collective-permute-done | bytes 552 | tf_op jit(solution)/shard_map/ppermute | solution.py:37
  (455 shorter events, 69.4 us)
Async XLA Ops:
  1.4 35.4 %copy-start.1 = (s32[16384]{0:T(1024)S(1)}, s32[16384]{0:T(1024)}, u32[]{:S(2)}) copy-start(s32[16384]{0:T(1024)} %param.15) | copy-start | bytes 196612
  29.8 9.2 %collective-permute-start.1 = (f32[128,256]{1,0:T(8,128)S(1)}, f32[128,256]{1,0:T(8,128)S(1)}, u32[]{:S(2)}, u32[]{:S(2)}) collective-permute-start(f32[128,256]{1,0:T(8,128)S(1)} %get-tuple-element.358), channel_id=1, source_target_pairs={{0,1},{1,2},{2,3},{3,4},{4,5},{5,6},{6,7},{7,8},{8,9},{9,10},{10,1... | collective-permute-start | bytes 393224 | tf_op jit(solution)/shard_map/ppermute | solution.py:16
  33.3 46.9 %collective-permute-start = (f32[128,256]{1,0:T(8,128)S(1)}, f32[128,256]{1,0:T(8,128)S(1)}, u32[]{:S(2)}, u32[]{:S(2)}) collective-permute-start(f32[128,256]{1,0:T(8,128)S(1)} %get-tuple-element.357), channel_id=1, source_target_pairs={{0,1},{1,2},{2,3},{3,4},{4,5},{5,6},{6,7},{7,8},{8,9},{9,10},{10,1... | collective-permute-start | bytes 393224 | tf_op jit(solution)/shard_map/ppermute | solution.py:16
  39.0 41.2 %collective-permute-start.2 = (f32[128,256]{1,0:T(8,128)S(1)}, f32[128,256]{1,0:T(8,128)S(1)}, u32[]{:S(2)}, u32[]{:S(2)}) collective-permute-start(f32[128,256]{1,0:T(8,128)S(1)} %slice_add_fusion), channel_id=1, source_target_pairs={{0,16},{16,32},{32,48},{48,64},{64,80},{80,96},{96,112},{112,128},... | collective-permute-start | bytes 393224 | tf_op jit(solution)/shard_map/ppermute | solution.py:16
  137.9 40.4 %copy-start = (f32[128,256]{1,0:T(8,128)}, f32[128,256]{1,0:T(8,128)S(1)}, u32[]{:S(2)}) copy-start(f32[128,256]{1,0:T(8,128)S(1)} %get-tuple-element.343) | copy-start | bytes 393220
  137.9 4.8 %collective-permute-start.3 = (f32[1,256]{1,0:T(1,128)S(1)}, f32[1,256]{1,0:T(1,128)S(1)}, u32[]{:S(2)}, u32[]{:S(2)}) collective-permute-start(f32[1,256]{1,0:T(1,128)S(1)} %get-tuple-element.382), channel_id=1, source_target_pairs={{16,0},{32,16},{48,32},{64,48},{80,64},{96,80},{112,96},{128,112},... | collective-permute-start | bytes 3080 | tf_op jit(solution)/shard_map/ppermute | solution.py:40
  140.8 6.1 %collective-permute-start.4 = (f32[1,256]{1,0:T(1,128)S(1)}, f32[1,256]{1,0:T(1,128)S(1)}, u32[]{:S(2)}, u32[]{:S(2)}) collective-permute-start(f32[1,256]{1,0:T(1,128)S(1)} %get-tuple-element.381), channel_id=1, source_target_pairs={{0,16},{16,32},{32,48},{48,64},{64,80},{80,96},{96,112},{112,128},... | collective-permute-start | bytes 3080 | tf_op jit(solution)/shard_map/ppermute | solution.py:37
  147.0 6.5 %collective-permute-start.5 = (f32[130,1]{1,0:T(8,128)S(1)}, f32[130,1]{1,0:T(8,128)S(1)}, u32[]{:S(2)}, u32[]{:S(2)}) collective-permute-start(f32[130,1]{1,0:T(8,128)S(1)} %get-tuple-element.369), channel_id=1, source_target_pairs={{1,0},{2,1},{3,2},{4,3},{5,4},{6,5},{7,6},{8,7},{9,8},{10,9},{11,1... | collective-permute-start | bytes 1568 | tf_op jit(solution)/shard_map/ppermute | solution.py:40
  151.6 8.3 %collective-permute-start.6 = (f32[130,1]{1,0:T(8,128)S(1)}, f32[130,1]{1,0:T(8,128)S(1)}, u32[]{:S(2)}, u32[]{:S(2)}) collective-permute-start(f32[130,1]{1,0:T(8,128)S(1)} %get-tuple-element.370), channel_id=1, source_target_pairs={{0,1},{1,2},{2,3},{3,4},{4,5},{5,6},{6,7},{7,8},{8,9},{9,10},{10,1... | collective-permute-start | bytes 1568 | tf_op jit(solution)/shard_map/ppermute | solution.py:37
  160.1 4.3 %collective-permute-start.7 = (f32[1,256]{1,0:T(1,128)S(1)}, f32[1,256]{1,0:T(1,128)S(1)}, u32[]{:S(2)}, u32[]{:S(2)}) collective-permute-start(f32[1,256]{1,0:T(1,128)S(1)} %get-tuple-element.380), channel_id=1, source_target_pairs={{16,0},{32,16},{48,32},{64,48},{80,64},{96,80},{112,96},{128,112},... | collective-permute-start | bytes 3080 | tf_op jit(solution)/shard_map/ppermute | solution.py:40
  162.0 6.1 %collective-permute-start.8 = (f32[1,256]{1,0:T(1,128)S(1)}, f32[1,256]{1,0:T(1,128)S(1)}, u32[]{:S(2)}, u32[]{:S(2)}) collective-permute-start(f32[1,256]{1,0:T(1,128)S(1)} %get-tuple-element.379), channel_id=1, source_target_pairs={{0,16},{16,32},{32,48},{48,64},{64,80},{80,96},{96,112},{112,128},... | collective-permute-start | bytes 3080 | tf_op jit(solution)/shard_map/ppermute | solution.py:37
  168.2 8.3 %collective-permute-start.10 = (f32[130,1]{1,0:T(8,128)S(1)}, f32[130,1]{1,0:T(8,128)S(1)}, u32[]{:S(2)}, u32[]{:S(2)}) collective-permute-start(f32[130,1]{1,0:T(8,128)S(1)} %get-tuple-element.368), channel_id=1, source_target_pairs={{0,1},{1,2},{2,3},{3,4},{4,5},{5,6},{6,7},{7,8},{8,9},{9,10},{10,1... | collective-permute-start | bytes 1568 | tf_op jit(solution)/shard_map/ppermute | solution.py:37
  170.1 8.0 %collective-permute-start.9 = (f32[130,1]{1,0:T(8,128)S(1)}, f32[130,1]{1,0:T(8,128)S(1)}, u32[]{:S(2)}, u32[]{:S(2)}) collective-permute-start(f32[130,1]{1,0:T(8,128)S(1)} %get-tuple-element.367), channel_id=1, source_target_pairs={{1,0},{2,1},{3,2},{4,3},{5,4},{6,5},{7,6},{8,7},{9,8},{10,9},{11,1... | collective-permute-start | bytes 1568 | tf_op jit(solution)/shard_map/ppermute | solution.py:40
  178.3 4.3 %collective-permute-start.11 = (f32[1,256]{1,0:T(1,128)S(1)}, f32[1,256]{1,0:T(1,128)S(1)}, u32[]{:S(2)}, u32[]{:S(2)}) collective-permute-start(f32[1,256]{1,0:T(1,128)S(1)} %get-tuple-element.378), channel_id=1, source_target_pairs={{16,0},{32,16},{48,32},{64,48},{80,64},{96,80},{112,96},{128,112},... | collective-permute-start | bytes 3080 | tf_op jit(solution)/shard_map/ppermute | solution.py:40
  180.2 6.1 %collective-permute-start.12 = (f32[1,256]{1,0:T(1,128)S(1)}, f32[1,256]{1,0:T(1,128)S(1)}, u32[]{:S(2)}, u32[]{:S(2)}) collective-permute-start(f32[1,256]{1,0:T(1,128)S(1)} %get-tuple-element.377), channel_id=1, source_target_pairs={{0,16},{16,32},{32,48},{48,64},{64,80},{80,96},{96,112},{112,128},... | collective-permute-start | bytes 3080 | tf_op jit(solution)/shard_map/ppermute | solution.py:37
  186.4 8.3 %collective-permute-start.13 = (f32[130,1]{1,0:T(8,128)S(1)}, f32[130,1]{1,0:T(8,128)S(1)}, u32[]{:S(2)}, u32[]{:S(2)}) collective-permute-start(f32[130,1]{1,0:T(8,128)S(1)} %get-tuple-element.365), channel_id=1, source_target_pairs={{1,0},{2,1},{3,2},{4,3},{5,4},{6,5},{7,6},{8,7},{9,8},{10,9},{11,1... | collective-permute-start | bytes 1568 | tf_op jit(solution)/shard_map/ppermute | solution.py:40
  192.8 8.3 %collective-permute-start.14 = (f32[130,1]{1,0:T(8,128)S(1)}, f32[130,1]{1,0:T(8,128)S(1)}, u32[]{:S(2)}, u32[]{:S(2)}) collective-permute-start(f32[130,1]{1,0:T(8,128)S(1)} %get-tuple-element.366), channel_id=1, source_target_pairs={{0,1},{1,2},{2,3},{3,4},{4,5},{5,6},{6,7},{7,8},{8,9},{9,10},{10,1... | collective-permute-start | bytes 1568 | tf_op jit(solution)/shard_map/ppermute | solution.py:37
  201.3 4.3 %collective-permute-start.15 = (f32[1,256]{1,0:T(1,128)S(1)}, f32[1,256]{1,0:T(1,128)S(1)}, u32[]{:S(2)}, u32[]{:S(2)}) collective-permute-start(f32[1,256]{1,0:T(1,128)S(1)} %get-tuple-element.376), channel_id=1, source_target_pairs={{16,0},{32,16},{48,32},{64,48},{80,64},{96,80},{112,96},{128,112},... | collective-permute-start | bytes 3080 | tf_op jit(solution)/shard_map/ppermute | solution.py:40
  203.2 6.1 %collective-permute-start.16 = (f32[1,256]{1,0:T(1,128)S(1)}, f32[1,256]{1,0:T(1,128)S(1)}, u32[]{:S(2)}, u32[]{:S(2)}) collective-permute-start(f32[1,256]{1,0:T(1,128)S(1)} %get-tuple-element.375), channel_id=1, source_target_pairs={{0,16},{16,32},{32,48},{48,64},{64,80},{80,96},{96,112},{112,128},... | collective-permute-start | bytes 3080 | tf_op jit(solution)/shard_map/ppermute | solution.py:37
  209.4 6.2 %collective-permute-start.17 = (f32[130,1]{1,0:T(8,128)S(1)}, f32[130,1]{1,0:T(8,128)S(1)}, u32[]{:S(2)}, u32[]{:S(2)}) collective-permute-start(f32[130,1]{1,0:T(8,128)S(1)} %get-tuple-element.363), channel_id=1, source_target_pairs={{1,0},{2,1},{3,2},{4,3},{5,4},{6,5},{7,6},{8,7},{9,8},{10,9},{11,1... | collective-permute-start | bytes 1568 | tf_op jit(solution)/shard_map/ppermute | solution.py:40
  211.4 8.3 %collective-permute-start.18 = (f32[130,1]{1,0:T(8,128)S(1)}, f32[130,1]{1,0:T(8,128)S(1)}, u32[]{:S(2)}, u32[]{:S(2)}) collective-permute-start(f32[130,1]{1,0:T(8,128)S(1)} %get-tuple-element.364), channel_id=1, source_target_pairs={{0,1},{1,2},{2,3},{3,4},{4,5},{5,6},{6,7},{7,8},{8,9},{9,10},{10,1... | collective-permute-start | bytes 1568 | tf_op jit(solution)/shard_map/ppermute | solution.py:37
  219.8 4.3 %collective-permute-start.19 = (f32[1,256]{1,0:T(1,128)S(1)}, f32[1,256]{1,0:T(1,128)S(1)}, u32[]{:S(2)}, u32[]{:S(2)}) collective-permute-start(f32[1,256]{1,0:T(1,128)S(1)} %get-tuple-element.374), channel_id=1, source_target_pairs={{16,0},{32,16},{48,32},{64,48},{80,64},{96,80},{112,96},{128,112},... | collective-permute-start | bytes 3080 | tf_op jit(solution)/shard_map/ppermute | solution.py:40
  221.8 6.1 %collective-permute-start.20 = (f32[1,256]{1,0:T(1,128)S(1)}, f32[1,256]{1,0:T(1,128)S(1)}, u32[]{:S(2)}, u32[]{:S(2)}) collective-permute-start(f32[1,256]{1,0:T(1,128)S(1)} %get-tuple-element.373), channel_id=1, source_target_pairs={{0,16},{16,32},{32,48},{48,64},{64,80},{80,96},{96,112},{112,128},... | collective-permute-start | bytes 3080 | tf_op jit(solution)/shard_map/ppermute | solution.py:37
  228.0 6.2 %collective-permute-start.21 = (f32[130,1]{1,0:T(8,128)S(1)}, f32[130,1]{1,0:T(8,128)S(1)}, u32[]{:S(2)}, u32[]{:S(2)}) collective-permute-start(f32[130,1]{1,0:T(8,128)S(1)} %get-tuple-element.361), channel_id=1, source_target_pairs={{1,0},{2,1},{3,2},{4,3},{5,4},{6,5},{7,6},{8,7},{9,8},{10,9},{11,1... | collective-permute-start | bytes 1568 | tf_op jit(solution)/shard_map/ppermute | solution.py:40
  229.9 8.3 %collective-permute-start.22 = (f32[130,1]{1,0:T(8,128)S(1)}, f32[130,1]{1,0:T(8,128)S(1)}, u32[]{:S(2)}, u32[]{:S(2)}) collective-permute-start(f32[130,1]{1,0:T(8,128)S(1)} %get-tuple-element.362), channel_id=1, source_target_pairs={{0,1},{1,2},{2,3},{3,4},{4,5},{5,6},{6,7},{7,8},{8,9},{9,10},{10,1... | collective-permute-start | bytes 1568 | tf_op jit(solution)/shard_map/ppermute | solution.py:37
  238.4 4.3 %collective-permute-start.23 = (f32[1,256]{1,0:T(1,128)S(1)}, f32[1,256]{1,0:T(1,128)S(1)}, u32[]{:S(2)}, u32[]{:S(2)}) collective-permute-start(f32[1,256]{1,0:T(1,128)S(1)} %get-tuple-element.372), channel_id=1, source_target_pairs={{16,0},{32,16},{48,32},{64,48},{80,64},{96,80},{112,96},{128,112},... | collective-permute-start | bytes 3080 | tf_op jit(solution)/shard_map/ppermute | solution.py:40
  240.3 6.1 %collective-permute-start.24 = (f32[1,256]{1,0:T(1,128)S(1)}, f32[1,256]{1,0:T(1,128)S(1)}, u32[]{:S(2)}, u32[]{:S(2)}) collective-permute-start(f32[1,256]{1,0:T(1,128)S(1)} %get-tuple-element.371), channel_id=1, source_target_pairs={{0,16},{16,32},{32,48},{48,64},{64,80},{80,96},{96,112},{112,128},... | collective-permute-start | bytes 3080 | tf_op jit(solution)/shard_map/ppermute | solution.py:37
  246.5 6.2 %collective-permute-start.25 = (f32[130,1]{1,0:T(8,128)S(1)}, f32[130,1]{1,0:T(8,128)S(1)}, u32[]{:S(2)}, u32[]{:S(2)}) collective-permute-start(f32[130,1]{1,0:T(8,128)S(1)} %get-tuple-element.359), channel_id=1, source_target_pairs={{1,0},{2,1},{3,2},{4,3},{5,4},{6,5},{7,6},{8,7},{9,8},{10,9},{11,1... | collective-permute-start | bytes 1568 | tf_op jit(solution)/shard_map/ppermute | solution.py:40
  248.4 8.3 %collective-permute-start.26 = (f32[130,1]{1,0:T(8,128)S(1)}, f32[130,1]{1,0:T(8,128)S(1)}, u32[]{:S(2)}, u32[]{:S(2)}) collective-permute-start(f32[130,1]{1,0:T(8,128)S(1)} %get-tuple-element.360), channel_id=1, source_target_pairs={{0,1},{1,2},{2,3},{3,4},{4,5},{5,6},{6,7},{7,8},{8,9},{9,10},{10,1... | collective-permute-start | bytes 1568 | tf_op jit(solution)/shard_map/ppermute | solution.py:37
where the time goes:
time: 261 us; the launch traced here: 258 us
  starting transfers between devices  75.6 us (29%)
  blocking collectives  54.3 us (21%)
  waiting for transfers between devices  52.6 us (20%)
  local copies, waits for them, and re-layouts  40 us (15%)
  matrix products  19.8 us (8%)
  other arithmetic  10 us (4%)
  loops' own time  4.05 us (2%)
    all_gather x2, blocking collectives, entering(): everything = lax.all_gather(value, axis)  54.3 us
    ppermute x12, waiting for transfers between devices, padded_2(): lax.ppermute(lax.slice_in_dim(block, block.shape[dim] - width, None, axis...  47.7 us
    ppermute x12, starting transfers between devices, padded_2(): lax.ppermute(lax.slice_in_dim(block, 0, width, axis=dim), axis, backward)  35.2 us
    ppermute x12, starting transfers between devices, padded_2(): lax.ppermute(lax.slice_in_dim(block, block.shape[dim] - width, None, axis...  31.5 us
    slice x32, local copies, waits for them, and re-layouts, area_add_block(): left = (rows == where[0][None, :]).astype(jnp.bfloat16)  24.8 us
    slice x16, local copies, waits for them, and re-layouts, impulse_add_block(): box[0][None, :]  13.6 us
    dot_general x32, matrix products, area_add_block(): jnp.dot(left, right, preferred_element_type=jnp.float32)  12.4 us
    ppermute x3, starting transfers between devices, from_behind(): return lax.ppermute(block, axis, route)  8.89 us
  transfers between devices with their start and end apart: 27, of which 17 were waited for; matrix products, arithmetic and copies ran while one was open for 15% of the time, Pallas kernels for 0%

commit v1 on v0

v1 whole, which is shorter than its diff:
```python
import jax
import jax.numpy as jnp
from jax import lax
from jax.experimental import pallas as pl
from jax.experimental.pallas import tpu as pltpu
from jax.sharding import PartitionSpec as P

BR = 128
BC = 256
STEPS = 6
TALL = 192
WIDE = 384
NET_BLOCK = 512
CELL_BLOCK = 1024
VMEM = pltpu.MemorySpace.VMEM


def rows_of(value, rows):
    return jnp.broadcast_to(value.astype(jnp.float32), (16, value.shape[1])).astype(jnp.bfloat16)[None]


def steps_of(rows, shift, n):
    base = lax.broadcasted_iota(jnp.int32, (rows // 16, 16, n), 0) * 16
    base = base + lax.broadcasted_iota(jnp.int32, (rows // 16, 16, n), 1) - shift
    return base.astype(jnp.float32).astype(jnp.bfloat16)


def lane_row(ref, first, n):
    return jnp.concatenate([ref[pl.ds(first // 128 + i, 1), :] for i in range(n // 128)], axis=1)


def nt_dot(left, right):
    return lax.dot_general(
        left, right, (((1,), (1,)), ((), ())), preferred_element_type=jnp.float32
    )


def window_kernel(place, boxes, pins, bins, area, d_out, a_out, right_out, left_out):
    row_first = place[0] * BR
    col_first = place[1] * BC
    zero = jnp.zeros((), jnp.bfloat16)
    one = jnp.ones((), jnp.bfloat16)
    n = NET_BLOCK
    demand = jnp.zeros((TALL, WIDE), jnp.float32)
    for k in range(4096 // n):
        box = boxes[:, k * n : (k + 1) * n]
        y0, y1, x0, x1 = (box[i : i + 1] for i in range(4))
        w = (x1 - x0 + 1).astype(jnp.float32)
        h = (y1 - y0 + 1).astype(jnp.float32)
        weight = lane_row(pins, k * n, n).astype(jnp.float32) * (w + h) / (w * h) / 16.0
        high = weight.astype(jnp.bfloat16)
        low = (weight - high.astype(jnp.float32)).astype(jnp.bfloat16)
        high = rows_of(high, 16)
        low = rows_of(low, 16)
        rows = steps_of(TALL, 0, n)
        inside = (rows >= rows_of(y0 - row_first, 16)) & (rows <= rows_of(y1 - row_first, 16))
        left = jnp.where(inside, one, zero).reshape(TALL, n)
        cols = steps_of(WIDE, 192, n)
        x0 = rows_of(x0 - (col_first + 192), 16)
        x1 = rows_of(x1 - (col_first + 192), 16)
        inside = (cols >= x0) & (cols <= x1)
        demand = demand + nt_dot(left, jnp.where(inside, high, zero).reshape(WIDE, n))
        demand = demand + nt_dot(left, jnp.where(inside, low, zero).reshape(WIDE, n))
    n = CELL_BLOCK
    total = jnp.zeros((BR, BC), jnp.float32)
    for k in range(16384 // n):
        where = bins[:, k * n : (k + 1) * n]
        left = steps_of(BR, 0, n) == rows_of(where[0:1] - row_first, 16)
        left = jnp.where(left, one, zero).reshape(BR, n)
        right = steps_of(BC, 0, n) == rows_of(where[1:2] - col_first, 16)
        right = jnp.where(right, rows_of(lane_row(area, k * n, n), 16), zero).reshape(BC, n)
        total = total + nt_dot(left, right)
    total = total * (1.0 / 16.0)
    d_out[...] = demand[:, :BC]
    a_out[...] = total
    right_out[:TALL] = demand[:, BC:]
    pad = jnp.zeros((64, 128), jnp.float32)
    edge = jnp.concatenate([demand[:, 128:BC], pad], axis=0).T[120:128]
    right_out[TALL : TALL + 8] = edge[:, :128]
    right_out[TALL + 8 : TALL + 16] = edge[:, 128:]
    right_out[TALL + 16 : TALL + 24] = total[:, 128:].T[120:128]
    edge = jnp.concatenate([demand[:, :128], pad], axis=0).T[:8]
    left_out[:8] = edge[:, :128]
    left_out[8:16] = edge[:, 128:]
    left_out[16:24] = total[:, :128].T[:8]


def stand(strip, at):
    length = strip.shape[1]
    parts = [strip]
    if at:
        parts = [jnp.zeros((at, length), jnp.float32)] + parts
    if at < 120:
        parts = parts + [jnp.zeros((120 - at, length), jnp.float32)]
    return jnp.concatenate(parts, axis=0).T


def merge_kernel(d_in, a_in, over, from_left, from_right, d_out, a_out, down_out, up_out):
    low = d_in[:, :128] + from_left[:TALL]
    mid = d_in[:, 128:]
    edge = jnp.concatenate([from_left[TALL : TALL + 8], from_left[TALL + 8 : TALL + 16]], axis=1)
    edge = stand(edge, 120)[:TALL]
    after = jnp.concatenate([from_right[:8], from_right[8:16]], axis=1)
    after = stand(after, 0)[:TALL]
    lane = lax.broadcasted_iota(jnp.int32, (TALL, 128), 1)
    high = jnp.where(lane < 6, over[:TALL] + after, jnp.where(lane >= 122, edge, 0.0))
    a_edge = stand(from_left[TALL + 16 :], 120)
    a_after = stand(from_right[16:], 0)
    lane = lane[:BR]
    a_high = jnp.where(lane < 6, a_after, jnp.where(lane >= 122, a_edge, 0.0))
    d_out[:, :128] = low[:BR]
    d_out[:, 128:256] = mid[:BR]
    d_out[:, 256:] = high[:BR]
    a_out[:, :256] = a_in[...]
    a_out[:, 256:] = a_high
    for i, block in enumerate((low, mid, high)):
        lanes = slice(128 * i, 128 * (i + 1))
        down_out[:64, lanes] = block[128:]
        down_out[64:72, lanes] = block[120:128]
        up_out[:8, lanes] = block[:8]
    down_out[72:80, :256] = a_in[120:128]
    down_out[72:80, 256:] = a_high[120:128]
    up_out[8:, :256] = a_in[:8]
    up_out[8:, 256:] = a_high[:8]


def final_kernel(place, d_in, a_in, over, from_above, from_below, demand_out, density_out):
    top = from_above[64:72]
    own = jnp.concatenate([d_in[:64] + from_above[:64], d_in[64:]], axis=0)
    bottom = over[...] + from_below[:8]
    demand_out[...] = own[:, :BC]
    demand = jnp.concatenate([top, own, bottom], axis=0)
    area = jnp.concatenate([from_above[72:80], a_in[...], from_below[8:]], axis=0)
    shape = demand.shape
    row = lax.broadcasted_iota(jnp.int32, shape, 0) - 8 + place[0] * BR
    lane = lax.broadcasted_iota(jnp.int32, shape, 1)
    col = jnp.where(lane < 320, lane, lane - WIDE)
    near = (col >= -6) & (col < BC + 6)
    col = col + place[1] * BC
    inside = near & (row >= 0) & (row < place[2]) & (col >= 0) & (col < place[3])
    start = (1.0 + 1.5 * demand / (1.0 + demand)) * area
    density = jnp.where(inside, start, 0.0)
    keep = jnp.where(inside, 0.04, 0.0)
    gain = jnp.where(inside, 0.24, 0.0)
    for _ in range(STEPS):
        beside = (
            pltpu.roll(density, 1, 0)
            + pltpu.roll(density, shape[0] - 1, 0)
            + pltpu.roll(density, 1, 1)
            + pltpu.roll(density, shape[1] - 1, 1)
        )
        density = keep * density + gain * beside
    density_out[...] = density[8 : 8 + BR, :BC]


def shift(block, axis, distance):
    devices = range(lax.axis_size(axis))
    route = [(i, i + distance) for i in devices if i + distance in devices]
    return lax.ppermute(block, axis, route)


def call(kernel, shapes, *args, scalars=0):
    specs = [pl.BlockSpec(memory_space=pltpu.MemorySpace.SMEM)] * scalars
    specs = specs + [pl.BlockSpec(memory_space=VMEM)] * (len(args) - scalars)
    return pl.pallas_call(
        kernel,
        out_shape=[jax.ShapeDtypeStruct(s, jnp.float32) for s in shapes],
        in_specs=specs,
        out_specs=[pl.BlockSpec(memory_space=VMEM)] * len(shapes),
        compiler_params=pltpu.CompilerParams(vmem_limit_bytes=48 * 2**20),
    )(*args)


def body(boxes, pins, cell_bins, cell_area):
    place = jnp.stack(
        [
            lax.axis_index("row"),
            lax.axis_index("col"),
            lax.axis_size("row") * BR,
            lax.axis_size("col") * BC,
        ]
    ).astype(jnp.int32)
    d_own, a_own, right, left = call(
        window_kernel,
        [(TALL, BC), (BR, BC), (TALL + 24, 128), (24, 128)],
        place,
        boxes,
        pins.reshape(-1, 128),
        cell_bins,
        cell_area.reshape(-1, 128),
        scalars=1,
    )
    from_left = shift(right, "col", 1)
    from_right = shift(left, "col", -1)
    d_ext, a_ext, down, up = call(
        merge_kernel,
        [(BR, WIDE), (BR, WIDE), (80, WIDE), (16, WIDE)],
        d_own,
        a_own,
        right,
        from_left,
        from_right,
    )
    from_above = shift(down, "row", 1)
    from_below = shift(up, "row", -1)
    demand, density = call(
        final_kernel,
        [(BR, BC), (BR, BC)],
        place,
        d_ext,
        a_ext,
        down[:8],
        from_above,
        from_below,
        scalars=1,
    )
    return (demand, density)


def solution(mesh):
    return jax.shard_map(
        body,
        mesh=mesh,
        in_specs=(
            P(None, ("row", "col")),
            P(("row", "col")),
            P(None, ("row", "col")),
            P(("row", "col")),
        ),
        out_specs=(P("row", "col"), P("row", "col")),
        check_vma=False,
    )
```

time: 261 us -> 34.2 us (0.13)
  the two profiles are of different devices: /device:TPU:130 before, /device:TPU:123 now
where the time goes in v1:
time: 34.2 us; the launch traced here: 33.9 us
  starting transfers between devices  14 us (41%)
  waiting for transfers between devices  8.45 us (25%)
  Pallas kernels  7.44 us (22%)
  local copies, waits for them, and re-layouts  3.2 us (9%)
  between operations  0.71 us (2%)
    ppermute x4, starting transfers between devices, shift(): return lax.ppermute(block, axis, route)  14 us
    ppermute x4, waiting for transfers between devices, shift(): return lax.ppermute(block, axis, route)  8.45 us
    pallas_call x3, Pallas kernels, call(): pl.pallas_call(kernel, out_shape=[jax.ShapeDtypeStruct(s, jnp.float32) fo...  7.44 us
    unnamed x8, local copies, waits for them, and re-layouts  3.2 us
  transfers between devices with their start and end apart: 4, of which 2 were waited for; matrix products, arithmetic and copies ran while one was open for 0% of the time, Pallas kernels for 0%

profile of v1, /device:TPU:123, one launch (start us, length us, event | category | flops | bytes accessed | tf_op | source)
XLA Modules:
  0.0 33.9 jit_solution(15178509648154777421)
XLA Ops:
  0.6 0.0 copy-start.3
  0.7 0.1 pad_add_fusion.place
  0.7 0.6 %copy-done.3 = s32[4096]{0:T(1024)S(1)} copy-done((s32[4096]{0:T(1024)S(1)}, s32[4096]{0:T(1024)}, u32[]{:S(2)}) %copy-start.3) | copy-done | bytes 16408
  1.3 0.0 copy-start
  1.4 0.9 %copy-done = s32[2,16384]{1,0:T(2,128)S(1)} copy-done((s32[2,16384]{1,0:T(2,128)S(1)}, s32[2,16384]{1,0:T(2,128)}, u32[]{:S(2)}) %copy-start) | copy-done | bytes 131096
  2.3 0.0 copy-start.1
  2.3 0.8 %copy-done.1 = s32[4,4096]{1,0:T(4,128)S(1)} copy-done((s32[4,4096]{1,0:T(4,128)S(1)}, s32[4,4096]{1,0:T(4,128)}, u32[]{:S(2)}) %copy-start.1) | copy-done | bytes 65560
  3.1 0.0 copy-start.2
  3.1 0.8 %copy-done.2 = s32[16384]{0:T(1024)S(1)} copy-done((s32[16384]{0:T(1024)S(1)}, s32[16384]{0:T(1024)}, u32[]{:S(2)}) %copy-start.2) | copy-done | bytes 65560
  3.9 5.1 %shard_map.59 = (f32[192,256]{1,0:T(8,128)S(1)}, f32[128,256]{1,0:T(8,128)S(1)}, f32[216,128]{1,0:T(8,128)S(1)}, f32[24,128]{1,0:T(8,128)S(1)}) custom-call(s32[4]{0:T(128)S(1)} %pad_add_fusion.place, s32[4,4096]{1,0:T(4,128)S(1)} %copy-done.1, s32[32,128]{1,0:T(8,128)S(1)} %bitcast.5, s32[2,16384]{1,0:T(2,128)S(1)} %copy-done, s32[128,128]{1,0:T(8,128)S(1)} %bitcast.4), custom_call_target="tpu_custom_call" | custom-call | tf_op jit(solution)/shard_map/pallas_call | solution.py:165
  9.0 2.8 %collective-permute-start = (f32[216,128]{1,0:T(8,128)S(1)}, f32[216,128]{1,0:T(8,128)S(1)}, u32[]{:S(2)}, u32[]{:S(2)}) collective-permute-start(f32[216,128]{1,0:T(8,128)S(1)} %get-tuple-element.12.over), channel_id=1, source_target_pairs={{0,1},{1,2},{2,3},{3,4},{4,5},{5,6},{6,7},{7,8},{8,9},{9,10},{10,1... | collective-permute-start | bytes 331784 | tf_op jit(solution)/shard_map/ppermute | solution.py:159
  11.8 2.5 %collective-permute-start.1 = (f32[24,128]{1,0:T(8,128)S(1)}, f32[24,128]{1,0:T(8,128)S(1)}, u32[]{:S(2)}, u32[]{:S(2)}) collective-permute-start(f32[24,128]{1,0:T(8,128)S(1)} %get-tuple-element.13), channel_id=1, source_target_pairs={{1,0},{2,1},{3,2},{4,3},{5,4},{6,5},{7,6},{8,7},{9,8},{10,9},{11,1... | collective-permute-start | bytes 36872 | tf_op jit(solution)/shard_map/ppermute | solution.py:159
  14.3 4.0 %collective-permute-done.1.from_right = f32[24,128]{1,0:T(8,128)S(1)} collective-permute-done((f32[24,128]{1,0:T(8,128)S(1)}, f32[24,128]{1,0:T(8,128)S(1)}, u32[]{:S(2)}, u32[]{:S(2)}) %collective-permute-start.1) | collective-permute-done | bytes 12320 | tf_op jit(solution)/shard_map/ppermute | solution.py:159
  18.4 0.0 collective-permute-done.from_left
  18.4 0.2 shard_map.60
  18.5 6.8 %collective-permute-start.2 = (f32[80,384]{1,0:T(8,128)S(1)}, f32[80,384]{1,0:T(8,128)S(1)}, u32[]{:S(2)}, u32[]{:S(2)}) collective-permute-start(f32[80,384]{1,0:T(8,128)S(1)} %get-tuple-element.16), channel_id=1, source_target_pairs={{0,16},{16,32},{32,48},{48,64},{64,80},{80,96},{96,112},{112,128},... | collective-permute-start | bytes 368648 | tf_op jit(solution)/shard_map/ppermute | solution.py:159
  25.3 1.9 %collective-permute-start.3 = (f32[16,384]{1,0:T(8,128)S(1)}, f32[16,384]{1,0:T(8,128)S(1)}, u32[]{:S(2)}, u32[]{:S(2)}) collective-permute-start(f32[16,384]{1,0:T(8,128)S(1)} %get-tuple-element.17), channel_id=1, source_target_pairs={{16,0},{32,16},{48,32},{64,48},{80,64},{96,80},{112,96},{128,112},... | collective-permute-start | bytes 73736 | tf_op jit(solution)/shard_map/ppermute | solution.py:159
  27.2 4.4 %collective-permute-done.3.from_below = f32[16,384]{1,0:T(8,128)S(1)} collective-permute-done((f32[16,384]{1,0:T(8,128)S(1)}, f32[16,384]{1,0:T(8,128)S(1)}, u32[]{:S(2)}, u32[]{:S(2)}) %collective-permute-start.3) | collective-permute-done | bytes 24608 | tf_op jit(solution)/shard_map/ppermute | solution.py:159
  31.7 0.0 collective-permute-done.2.from_above
  31.7 2.2 %shard_map.61 = (f32[128,256]{1,0:T(8,128)}, f32[128,256]{1,0:T(8,128)}) custom-call(s32[4]{0:T(128)S(1)} %pad_add_fusion.place, f32[128,384]{1,0:T(8,128)S(1)} %get-tuple-element.14.d_in, f32[128,384]{1,0:T(8,128)S(1)} %get-tuple-element.15.a_in, f32[8,384]{1,0:T(8,128)S(1)} %slice.3.over, f32[80,384]{1,0:T(8,128)S(1)} %collective-permute-done.2.from_above, ...), custom_call_target="tpu_custom_call" | custom-call | tf_op jit(solution)/shard_map/pallas_call | solution.py:165
  (2 shorter events, 0.0 us)
Async XLA Ops:
  0.6 0.7 %copy-start.3 = (s32[4096]{0:T(1024)S(1)}, s32[4096]{0:T(1024)}, u32[]{:S(2)}) copy-start(s32[4096]{0:T(1024)} %param.5) | copy-start | bytes 49156
  1.3 0.9 %copy-start = (s32[2,16384]{1,0:T(2,128)S(1)}, s32[2,16384]{1,0:T(2,128)}, u32[]{:S(2)}) copy-start(s32[2,16384]{1,0:T(2,128)} %bins.1) | copy-start | bytes 393220
  2.3 0.8 %copy-start.1 = (s32[4,4096]{1,0:T(4,128)S(1)}, s32[4,4096]{1,0:T(4,128)}, u32[]{:S(2)}) copy-start(s32[4,4096]{1,0:T(4,128)} %boxes.1) | copy-start | bytes 196612
  3.1 0.8 %copy-start.2 = (s32[16384]{0:T(1024)S(1)}, s32[16384]{0:T(1024)}, u32[]{:S(2)}) copy-start(s32[16384]{0:T(1024)} %param.7) | copy-start | bytes 196612
  9.0 9.3 %collective-permute-start = (f32[216,128]{1,0:T(8,128)S(1)}, f32[216,128]{1,0:T(8,128)S(1)}, u32[]{:S(2)}, u32[]{:S(2)}) collective-permute-start(f32[216,128]{1,0:T(8,128)S(1)} %get-tuple-element.12.over), channel_id=1, source_target_pairs={{0,1},{1,2},{2,3},{3,4},{4,5},{5,6},{6,7},{7,8},{8,9},{9,10},{10,1... | collective-permute-start | bytes 331784 | tf_op jit(solution)/shard_map/ppermute | solution.py:159
  11.8 6.5 %collective-permute-start.1 = (f32[24,128]{1,0:T(8,128)S(1)}, f32[24,128]{1,0:T(8,128)S(1)}, u32[]{:S(2)}, u32[]{:S(2)}) collective-permute-start(f32[24,128]{1,0:T(8,128)S(1)} %get-tuple-element.13), channel_id=1, source_target_pairs={{1,0},{2,1},{3,2},{4,3},{5,4},{6,5},{7,6},{8,7},{9,8},{10,9},{11,1... | collective-permute-start | bytes 36872 | tf_op jit(solution)/shard_map/ppermute | solution.py:159
  18.5 13.1 %collective-permute-start.2 = (f32[80,384]{1,0:T(8,128)S(1)}, f32[80,384]{1,0:T(8,128)S(1)}, u32[]{:S(2)}, u32[]{:S(2)}) collective-permute-start(f32[80,384]{1,0:T(8,128)S(1)} %get-tuple-element.16), channel_id=1, source_target_pairs={{0,16},{16,32},{32,48},{48,64},{64,80},{80,96},{96,112},{112,128},... | collective-permute-start | bytes 368648 | tf_op jit(solution)/shard_map/ppermute | solution.py:159
  25.3 6.4 %collective-permute-start.3 = (f32[16,384]{1,0:T(8,128)S(1)}, f32[16,384]{1,0:T(8,128)S(1)}, u32[]{:S(2)}, u32[]{:S(2)}) collective-permute-start(f32[16,384]{1,0:T(8,128)S(1)} %get-tuple-element.17), channel_id=1, source_target_pairs={{16,0},{32,16},{48,32},{64,48},{80,64},{96,80},{112,96},{128,112},... | collective-permute-start | bytes 73736 | tf_op jit(solution)/shard_map/ppermute | solution.py:159

commit v2 on v0

v2 whole, which is shorter than its diff:
```python
import jax
import jax.numpy as jnp
from jax import lax
from jax.experimental import pallas as pl
from jax.experimental.pallas import tpu as pltpu
from jax.sharding import PartitionSpec as P

BR = 128
BC = 256
STEPS = 6
TALL = 192
WIDE = 384
NET_BLOCK = 1024
CELL_BLOCK = 1024
FACTORS = 24
F32 = jnp.float32
BF16 = jnp.bfloat16
FP8 = jnp.float8_e4m3fn
VMEM = pltpu.MemorySpace.VMEM
HBM = pltpu.MemorySpace.HBM


def repeated(value, rows, dtype):
    if dtype != jnp.int8:
        value = value.astype(F32)
    return jnp.broadcast_to(value, (rows, value.shape[1])).astype(dtype)[None]


def ruler(length, rows, shift, n, dtype):
    shape = (length // rows, rows, n)
    place = lax.broadcasted_iota(jnp.int32, shape, 0) * rows
    place = place + lax.broadcasted_iota(jnp.int32, shape, 1) - shift
    return place.astype(dtype) if dtype == jnp.int8 else place.astype(F32).astype(dtype)


def lane_row(ref, first, n):
    return jnp.concatenate([ref[pl.ds(first // 128 + i, 1), :] for i in range(n // 128)], axis=1)


def nt_dot(left, right):
    return lax.dot_general(left, right, (((1,), (1,)), ((), ())), preferred_element_type=F32)


def split_weights(boxes, pins, row_factor, col_factor):
    width = boxes[3:4, :] - boxes[2:3, :] + 1
    height = boxes[1:2, :] - boxes[0:1, :] + 1
    nets = width.shape[1]
    width, height = (
        jnp.concatenate([v[:, i : i + 128] for i in range(0, nets, 128)], axis=0).astype(F32)
        for v in (width, height)
    )
    weight = pins[...].astype(F32) * (width + height) / (width * height) * (1.0 / 16.0)
    best = weight
    for k in range(FACTORS):
        one = 1.0 + k / 128.0
        other = (weight * (1.0 / one)).astype(BF16).astype(F32)
        error = jnp.abs(other * one - weight)
        if k == 0:
            best, row_part, col_part = error, jnp.ones_like(weight), other
        else:
            better = error < best
            best = jnp.where(better, error, best)
            row_part = jnp.where(better, one, row_part)
            col_part = jnp.where(better, other, col_part)
    row_factor[...] = row_part
    col_factor[...] = col_part


def window_kernel(
    boxes_in, pins_in, bins_in, area_in, d_out, a_out, even_out, odd_out,
    boxes, pins, bins, area, row_factor, col_factor, sems,
):
    copies = [
        pltpu.make_async_copy(source, target, sems.at[i])
        for i, (source, target) in enumerate(
            ((boxes_in, boxes), (pins_in, pins), (bins_in, bins), (area_in, area))
        )
    ]
    for copy in copies:
        copy.start()
    copies[0].wait()
    copies[1].wait()
    split_weights(boxes, pins, row_factor, col_factor)
    n = NET_BLOCK
    zero = jnp.zeros((), BF16)
    demand = jnp.zeros((WIDE, TALL), F32)
    for k in range(0, boxes.shape[1], n):
        box = boxes[:, k : k + n]
        y0, y1, x0, x1 = (box[i : i + 1] for i in range(4))
        top = y0 & (BR - 1)
        bottom = y1 - (y0 - top)
        start = x0 & (BC - 1)
        end = x1 - (x0 - start)
        rows = ruler(TALL, 16, 0, n, BF16)
        inside = (rows >= repeated(top, 16, BF16)) & (rows <= repeated(bottom, 16, BF16))
        down = jnp.where(inside, repeated(lane_row(row_factor, k, n), 16, BF16), zero)
        cols = ruler(WIDE, 16, 192, n, BF16)
        inside = (cols >= repeated(start - 192, 16, BF16)) & (
            cols <= repeated(end - 192, 16, BF16)
        )
        right = jnp.where(inside, repeated(lane_row(col_factor, k, n), 16, BF16), zero)
        demand = demand + nt_dot(right.reshape(WIDE, n), down.reshape(TALL, n))
    copies[2].wait()
    copies[3].wait()
    n = CELL_BLOCK
    zero = jnp.zeros((), FP8)
    one = jnp.ones((), FP8)
    total = jnp.zeros((BC, 2 * BR), F32)
    for k in range(0, bins.shape[1], n):
        where = bins[:, k : k + n]
        size = lane_row(area, k, n)
        rows = ruler(BR, 32, 0, n, jnp.int8) == repeated(where[0:1] & (BR - 1), 32, jnp.int8)
        down = jnp.concatenate(
            [
                jnp.where(rows, repeated(part, 32, FP8), zero).reshape(BR, n)
                for part in (size >> 3, size & 7)
            ],
            axis=0,
        )
        cols = ruler(BC, 32, 128, n, jnp.int8) == repeated(
            (where[1:2] & (BC - 1)) - 128, 32, jnp.int8
        )
        right = jnp.where(cols, one, zero).reshape(BC, n)
        total = total + nt_dot(right, down)
    demand = demand.T
    total = (total[:, :BR] * 0.5 + total[:, BR:] * (1.0 / 16.0)).T
    d_out[...] = demand[: BR + 8]
    a_out[...] = total
    even = lax.rem(lax.axis_index("row"), 2) == 0
    for message, goes_down in ((even_out, even), (odd_out, jnp.logical_not(even))):
        message[:8] = jnp.where(goes_down, demand[BR : BR + 8], demand[:8])
        message[8:64] = demand[BR + 8 :]
        message[64:72] = demand[BR - 8 : BR]
        message[72:, :BC] = jnp.where(goes_down, total[BR - 8 :], total[:8])


def merge_kernel(d_own, a_own, even_in, odd_in, d_out, a_out, even_out, odd_out):
    even = lax.rem(lax.axis_index("row"), 2) == 0
    above = jnp.where(even, odd_in[...], even_in[...])
    below = jnp.where(even, even_in[:8], odd_in[:8])
    below_area = jnp.where(even, even_in[72:, :BC], odd_in[72:, :BC])
    demand = jnp.concatenate(
        [d_own[:64] + above[:64], d_own[64:BR], d_own[BR:] + below, above[64:72]], axis=0
    )
    area = jnp.concatenate([a_own[...], below_area, above[72:, :BC]], axis=0)
    d_out[...] = demand
    a_out[...] = area
    lane = lax.broadcasted_iota(jnp.int32, (BR + 16, 128), 1)
    leftward = jnp.where(lane < 8, demand[:, :128], pltpu.roll(area[:, :128], 8, 1))
    strip = jnp.where(lane < 120, pltpu.roll(demand[:, 128:BC], 120, 1), area[:, 128:])
    strip = jnp.concatenate([strip, jnp.zeros((112, 128), F32)], axis=0).T[112:]
    even = lax.rem(lax.axis_index("col"), 2) == 0
    for message, goes_right in ((even_out, even), (odd_out, jnp.logical_not(even))):
        message[: BR + 16] = jnp.where(goes_right, demand[:, BC:], leftward)
        message[BR + 16 : BR + 32] = strip[:, :128]
        message[BR + 32 :] = strip[:, 128:]


def final_kernel(d_in, a_in, even_in, odd_in, demand_out, density_out):
    tall = BR + 16
    even = lax.rem(lax.axis_index("col"), 2) == 0
    left = jnp.where(even, odd_in[...], even_in[...])
    right = jnp.where(even, even_in[:tall], odd_in[:tall])
    strip = jnp.concatenate([left[tall : tall + 16], left[tall + 16 :]], axis=1)
    strip = jnp.concatenate([jnp.zeros((112, 256), F32), strip], axis=0).T[:tall]
    lane = lax.broadcasted_iota(jnp.int32, (tall, 128), 1)
    beyond = jnp.where(lane < 8, d_in[:, BC:] + right, pltpu.roll(strip, 8, 1))
    demand = jnp.concatenate([d_in[:, :128] + left[:tall], d_in[:, 128:BC], beyond], axis=1)
    beyond = jnp.where(lane < 8, pltpu.roll(right, 120, 1), strip)
    area = jnp.concatenate([a_in[...], beyond], axis=1)
    demand_out[...] = demand[:BR, :BC]
    shape = demand.shape
    row = lax.broadcasted_iota(jnp.int32, shape, 0)
    row = jnp.where(row < BR + 8, row, row - tall) + lax.axis_index("row") * BR
    lane = lax.broadcasted_iota(jnp.int32, shape, 1)
    near = (lane < BC + 8) | (lane >= WIDE - 8)
    col = jnp.where(lane < BC + 8, lane, lane - WIDE) + lax.axis_index("col") * BC
    rows, cols = lax.axis_size("row") * BR, lax.axis_size("col") * BC
    inside = near & (row >= 0) & (row < rows) & (col >= 0) & (col < cols)
    start = (1.0 + 1.5 * demand / (1.0 + demand)) * area
    density = jnp.where(inside, start, 0.0)
    keep = jnp.where(inside, 0.04, 0.0)
    gain = jnp.where(inside, 0.24, 0.0)
    for _ in range(STEPS):
        beside = (
            pltpu.roll(density, 1, 0)
            + pltpu.roll(density, shape[0] - 1, 0)
            + pltpu.roll(density, 1, 1)
            + pltpu.roll(density, shape[1] - 1, 1)
        )
        density = keep * density + gain * beside
    density_out[...] = density[:BR, :BC]


def swap(block, axis, first):
    pairs = range(first, lax.axis_size(axis) - 1, 2)
    return lax.ppermute(block, axis, [p for i in pairs for p in ((i, i + 1), (i + 1, i))])


def call(kernel, shapes, *args, space=VMEM, scratch=()):
    return pl.pallas_call(
        kernel,
        out_shape=[jax.ShapeDtypeStruct(s, F32) for s in shapes],
        in_specs=[pl.BlockSpec(memory_space=space)] * len(args),
        out_specs=[pl.BlockSpec(memory_space=VMEM)] * len(shapes),
        scratch_shapes=list(scratch),
        compiler_params=pltpu.CompilerParams(vmem_limit_bytes=40 * 2**20),
    )(*args)


def body(boxes, pins, cell_bins, cell_area):
    pins = pins.reshape(-1, 128)
    cell_area = cell_area.reshape(-1, 128)
    inputs = (boxes, pins, cell_bins, cell_area)
    inputs = [pltpu.with_memory_space_constraint(a, HBM) for a in inputs]
    d_own, a_own, even, odd = call(
        window_kernel,
        [(BR + 8, WIDE), (BR, BC), (80, WIDE), (80, WIDE)],
        *inputs,
        space=HBM,
        scratch=[pltpu.VMEM(a.shape, a.dtype) for a in inputs]
        + [pltpu.VMEM(pins.shape, F32)] * 2
        + [pltpu.SemaphoreType.DMA((4,))],
    )
    odd = swap(odd, "row", 1)
    even = swap(even, "row", 0)
    d_ext, a_ext, even, odd = call(
        merge_kernel,
        [(BR + 16, WIDE), (BR + 16, BC), (BR + 48, 128), (BR + 48, 128)],
        d_own,
        a_own,
        even,
        odd,
    )
    odd = swap(odd, "col", 1)
    even = swap(even, "col", 0)
    demand, density = call(final_kernel, [(BR, BC), (BR, BC)], d_ext, a_ext, even, odd)
    return (demand, density)


def solution(mesh):
    return jax.shard_map(
        body,
        mesh=mesh,
        in_specs=(
            P(None, ("row", "col")),
            P(("row", "col")),
            P(None, ("row", "col")),
            P(("row", "col")),
        ),
        out_specs=(P("row", "col"), P("row", "col")),
        check_vma=False,
    )
```

time: 261 us -> 29.2 us (0.11)
  the two profiles are of different devices: /device:TPU:130 before, /device:TPU:9 now
where the time goes in v2:
time: 29.2 us; the launch traced here: 29 us
  starting transfers between devices  15.4 us (53%)
  Pallas kernels  6.84 us (23%)
  waiting for transfers between devices  6.08 us (21%)
  between operations  0.69 us (2%)
    ppermute x4, starting transfers between devices, swap(): lax.ppermute(block, axis, [p for i in pairs for p in ((i, i + 1), (i + 1,...  15.4 us
    pallas_call x3, Pallas kernels, call(): pl.pallas_call(kernel, out_shape=[jax.ShapeDtypeStruct(s, F32) for s in s...  6.84 us
    ppermute x4, waiting for transfers between devices, swap(): lax.ppermute(block, axis, [p for i in pairs for p in ((i, i + 1), (i + 1,...  6.08 us
  transfers between devices with their start and end apart: 4, of which 2 were waited for; matrix products, arithmetic and copies ran while one was open for 0% of the time, Pallas kernels for 0%

profile of v2, /device:TPU:9, one launch (start us, length us, event | category | flops | bytes accessed | tf_op | source)
XLA Modules:
  0.0 29.0 jit_solution(6403159812051624082)
XLA Ops:
  0.6 4.9 %shard_map.59 = (f32[136,384]{1,0:T(8,128)S(1)}, f32[128,256]{1,0:T(8,128)S(1)}, f32[80,384]{1,0:T(8,128)S(1)}, f32[80,384]{1,0:T(8,128)S(1)}) custom-call(s32[4,4096]{1,0:T(4,128)} %boxes_in.1, s32[32,128]{1,0:T(8,128)} %bitcast.3, s32[2,16384]{1,0:T(2,128)} %bins_in.1, s32[128,128]{1,0:T(8,128)} %bitcast.2), custom_call_target="tpu_custom_call" | custom-call | tf_op jit(solution)/shard_map/pallas_call | solution.py:201
  5.5 2.6 %collective-permute-start = (f32[80,384]{1,0:T(8,128)S(1)}, f32[80,384]{1,0:T(8,128)S(1)}, u32[]{:S(2)}, u32[]{:S(2)}) collective-permute-start(f32[80,384]{1,0:T(8,128)S(1)} %get-tuple-element.12), channel_id=1, source_target_pairs={{0,16},{16,0},{32,48},{48,32},{64,80},{80,64},{96,112},{112,96},{1... | collective-permute-start | bytes 368648 | tf_op jit(solution)/shard_map/ppermute | solution.py:197
  8.1 3.4 %collective-permute-start.1 = (f32[80,384]{1,0:T(8,128)S(1)}, f32[80,384]{1,0:T(8,128)S(1)}, u32[]{:S(2)}, u32[]{:S(2)}) collective-permute-start(f32[80,384]{1,0:T(8,128)S(1)} %get-tuple-element.13), channel_id=1, source_target_pairs={{16,32},{32,16},{48,64},{64,48},{80,96},{96,80},{112,128},{128,112... | collective-permute-start | bytes 368648 | tf_op jit(solution)/shard_map/ppermute | solution.py:197
  11.5 0.0 collective-permute-done.even_in
  11.6 2.7 %collective-permute-done.1.odd_in = f32[80,384]{1,0:T(8,128)S(1)} collective-permute-done((f32[80,384]{1,0:T(8,128)S(1)}, f32[80,384]{1,0:T(8,128)S(1)}, u32[]{:S(2)}, u32[]{:S(2)}) %collective-permute-start.1) | collective-permute-done | bytes 122912 | tf_op jit(solution)/shard_map/ppermute | solution.py:197
  14.3 0.2 shard_map.60
  14.5 7.5 %collective-permute-start.2 = (f32[176,128]{1,0:T(8,128)S(1)}, f32[176,128]{1,0:T(8,128)S(1)}, u32[]{:S(2)}, u32[]{:S(2)}) collective-permute-start(f32[176,128]{1,0:T(8,128)S(1)} %get-tuple-element.16), channel_id=1, source_target_pairs={{0,1},{1,0},{2,3},{3,2},{4,5},{5,4},{6,7},{7,6},{8,9},{9,8},{10,11... | collective-permute-start | bytes 270344 | tf_op jit(solution)/shard_map/ppermute | solution.py:197
  21.9 1.9 %collective-permute-start.3 = (f32[176,128]{1,0:T(8,128)S(1)}, f32[176,128]{1,0:T(8,128)S(1)}, u32[]{:S(2)}, u32[]{:S(2)}) collective-permute-start(f32[176,128]{1,0:T(8,128)S(1)} %get-tuple-element.17), channel_id=1, source_target_pairs={{1,2},{2,1},{3,4},{4,3},{5,6},{6,5},{7,8},{8,7},{9,10},{10,9},{11,... | collective-permute-start | bytes 270344 | tf_op jit(solution)/shard_map/ppermute | solution.py:197
  23.9 0.0 collective-permute-done.2.even_in
  23.9 3.3 %collective-permute-done.3.odd_in = f32[176,128]{1,0:T(8,128)S(1)} collective-permute-done((f32[176,128]{1,0:T(8,128)S(1)}, f32[176,128]{1,0:T(8,128)S(1)}, u32[]{:S(2)}, u32[]{:S(2)}) %collective-permute-start.3) | collective-permute-done | bytes 90144 | tf_op jit(solution)/shard_map/ppermute | solution.py:197
  27.2 1.8 %shard_map.61 = (f32[128,256]{1,0:T(8,128)}, f32[128,256]{1,0:T(8,128)}) custom-call(f32[144,384]{1,0:T(8,128)S(1)} %get-tuple-element.14.d_in, f32[144,256]{1,0:T(8,128)S(1)} %get-tuple-element.15.a_in, f32[176,128]{1,0:T(8,128)S(1)} %collective-permute-done.2.even_in, f32[176,128]{1,0:T(8,128)S(1)} %collective-permute-done.3.odd_in), custom_call_target="tpu_custom_call" | custom-call | tf_op jit(solution)/shard_map/pallas_call | solution.py:201
Async XLA Ops:
  5.5 6.0 %collective-permute-start = (f32[80,384]{1,0:T(8,128)S(1)}, f32[80,384]{1,0:T(8,128)S(1)}, u32[]{:S(2)}, u32[]{:S(2)}) collective-permute-start(f32[80,384]{1,0:T(8,128)S(1)} %get-tuple-element.12), channel_id=1, source_target_pairs={{0,16},{16,0},{32,48},{48,32},{64,80},{80,64},{96,112},{112,96},{1... | collective-permute-start | bytes 368648 | tf_op jit(solution)/shard_map/ppermute | solution.py:197
  8.1 6.2 %collective-permute-start.1 = (f32[80,384]{1,0:T(8,128)S(1)}, f32[80,384]{1,0:T(8,128)S(1)}, u32[]{:S(2)}, u32[]{:S(2)}) collective-permute-start(f32[80,384]{1,0:T(8,128)S(1)} %get-tuple-element.13), channel_id=1, source_target_pairs={{16,32},{32,16},{48,64},{64,48},{80,96},{96,80},{112,128},{128,112... | collective-permute-start | bytes 368648 | tf_op jit(solution)/shard_map/ppermute | solution.py:197
  14.5 9.4 %collective-permute-start.2 = (f32[176,128]{1,0:T(8,128)S(1)}, f32[176,128]{1,0:T(8,128)S(1)}, u32[]{:S(2)}, u32[]{:S(2)}) collective-permute-start(f32[176,128]{1,0:T(8,128)S(1)} %get-tuple-element.16), channel_id=1, source_target_pairs={{0,1},{1,0},{2,3},{3,2},{4,5},{5,4},{6,7},{7,6},{8,9},{9,8},{10,11... | collective-permute-start | bytes 270344 | tf_op jit(solution)/shard_map/ppermute | solution.py:197
  21.9 5.3 %collective-permute-start.3 = (f32[176,128]{1,0:T(8,128)S(1)}, f32[176,128]{1,0:T(8,128)S(1)}, u32[]{:S(2)}, u32[]{:S(2)}) collective-permute-start(f32[176,128]{1,0:T(8,128)S(1)} %get-tuple-element.17), channel_id=1, source_target_pairs={{1,2},{2,1},{3,4},{4,3},{5,6},{6,5},{7,8},{8,7},{9,10},{10,9},{11,... | collective-permute-start | bytes 270344 | tf_op jit(solution)/shard_map/ppermute | solution.py:197

commit v3 on v2

--- a/solution.py
+++ b/solution.py
@@ -10,8 +10,8 @@
 STEPS = 6
 TALL = 192
 WIDE = 384
-NET_BLOCK = 1024
-CELL_BLOCK = 1024
+NET_BLOCK = 4096
+CELL_BLOCK = 8192
 FACTORS = 24
 F32 = jnp.float32
 BF16 = jnp.bfloat16
@@ -83,9 +83,10 @@
     split_weights(boxes, pins, row_factor, col_factor)
     n = NET_BLOCK
     zero = jnp.zeros((), BF16)
-    demand = jnp.zeros((WIDE, TALL), F32)
-    for k in range(0, boxes.shape[1], n):
-        box = boxes[:, k : k + n]
+
+    def add_nets(i, demand):
+        k = pl.multiple_of(i * n, n)
+        box = boxes[:, pl.ds(k, n)]
         y0, y1, x0, x1 = (box[i : i + 1] for i in range(4))
         top = y0 & (BR - 1)
         bottom = y1 - (y0 - top)
@@ -99,29 +100,34 @@
             cols <= repeated(end - 192, 16, BF16)
         )
         right = jnp.where(inside, repeated(lane_row(col_factor, k, n), 16, BF16), zero)
-        demand = demand + nt_dot(right.reshape(WIDE, n), down.reshape(TALL, n))
+        return demand + nt_dot(right.reshape(WIDE, n), down.reshape(TALL, n))
+
+    demand = lax.fori_loop(0, boxes.shape[1] // n, add_nets, jnp.zeros((WIDE, TALL), F32))
     copies[2].wait()
     copies[3].wait()
-    n = CELL_BLOCK
+    m = CELL_BLOCK
     zero = jnp.zeros((), FP8)
     one = jnp.ones((), FP8)
-    total = jnp.zeros((BC, 2 * BR), F32)
-    for k in range(0, bins.shape[1], n):
-        where = bins[:, k : k + n]
-        size = lane_row(area, k, n)
-        rows = ruler(BR, 32, 0, n, jnp.int8) == repeated(where[0:1] & (BR - 1), 32, jnp.int8)
+
+    def add_cells(i, total):
+        k = pl.multiple_of(i * m, m)
+        where = bins[:, pl.ds(k, m)]
+        size = lane_row(area, k, m)
+        rows = ruler(BR, 32, 0, m, jnp.int8) == repeated(where[0:1] & (BR - 1), 32, jnp.int8)
         down = jnp.concatenate(
             [
-                jnp.where(rows, repeated(part, 32, FP8), zero).reshape(BR, n)
+                jnp.where(rows, repeated(part, 32, FP8), zero).reshape(BR, m)
                 for part in (size >> 3, size & 7)
             ],
             axis=0,
         )
-        cols = ruler(BC, 32, 128, n, jnp.int8) == repeated(
+        cols = ruler(BC, 32, 128, m, jnp.int8) == repeated(
             (where[1:2] & (BC - 1)) - 128, 32, jnp.int8
         )
-        right = jnp.where(cols, one, zero).reshape(BC, n)
-        total = total + nt_dot(right, down)
+        right = jnp.where(cols, one, zero).reshape(BC, m)
+        return total + nt_dot(right, down)
+
+    total = lax.fori_loop(0, bins.shape[1] // m, add_cells, jnp.zeros((BC, 2 * BR), F32))
     demand = demand.T
     total = (total[:, :BR] * 0.5 + total[:, BR:] * (1.0 / 16.0)).T
     d_out[...] = demand[: BR + 8]
@@ -134,7 +140,7 @@
         message[72:, :BC] = jnp.where(goes_down, total[BR - 8 :], total[:8])
 
 
-def merge_kernel(d_own, a_own, even_in, odd_in, d_out, a_out, even_out, odd_out):
+def merge_kernel(d_own, a_own, odd_in, even_in, d_out, a_out, even_out, odd_out):
     even = lax.rem(lax.axis_index("row"), 2) == 0
     above = jnp.where(even, odd_in[...], even_in[...])
     below = jnp.where(even, even_in[:8], odd_in[:8])
@@ -156,7 +162,9 @@
         message[BR + 32 :] = strip[:, 128:]
 
 
-def final_kernel(d_in, a_in, even_in, odd_in, demand_out, density_out):
+def final_kernel(
+    d_in, a_in, odd_in, even_in, demand_out, density_out, whole, own, field, inner, sems
+):
     tall = BR + 16
     even = lax.rem(lax.axis_index("col"), 2) == 0
     left = jnp.where(even, odd_in[...], even_in[...])
@@ -168,7 +176,9 @@
     demand = jnp.concatenate([d_in[:, :128] + left[:tall], d_in[:, 128:BC], beyond], axis=1)
     beyond = jnp.where(lane < 8, pltpu.roll(right, 120, 1), strip)
     area = jnp.concatenate([a_in[...], beyond], axis=1)
-    demand_out[...] = demand[:BR, :BC]
+    whole[...] = demand[:BR, :BC]
+    sent = pltpu.make_async_copy(whole, demand_out, sems.at[0])
+    sent.start()
     shape = demand.shape
     row = lax.broadcasted_iota(jnp.int32, shape, 0)
     row = jnp.where(row < BR + 8, row, row - tall) + lax.axis_index("row") * BR
@@ -179,17 +189,39 @@
     inside = near & (row >= 0) & (row < rows) & (col >= 0) & (col < cols)
     start = (1.0 + 1.5 * demand / (1.0 + demand)) * area
     density = jnp.where(inside, start, 0.0)
-    keep = jnp.where(inside, 0.04, 0.0)
-    gain = jnp.where(inside, 0.24, 0.0)
+    mask = jnp.where(inside, 1.0, 0.0)
+    for i in range(3):
+        field[i] = density[:, 128 * i : 128 * (i + 1)]
+        inner[i] = mask[:, 128 * i : 128 * (i + 1)]
+    part = shape[0] // 8
+
+    def strided(ref, k):
+        return jnp.concatenate([ref[i, pl.ds(k, 8, stride=part), :] for i in range(3)], axis=1)
+
+    block = [strided(field, k) for k in range(part)]
+
+    def step(_, block):
+        first = pltpu.roll(block[-1], 1, 0)
+        last = pltpu.roll(block[0], 7, 0)
+        rows = [first, *block, last]
+        new = []
+        for k in range(part):
+            mid = rows[k + 1]
+            beside = rows[k] + rows[k + 2] + pltpu.roll(mid, 1, 1) + pltpu.roll(mid, WIDE - 1, 1)
+            new.append(strided(inner, k) * (0.04 * mid + 0.24 * beside))
+        return tuple(new)
+
     for _ in range(STEPS):
-        beside = (
-            pltpu.roll(density, 1, 0)
-            + pltpu.roll(density, shape[0] - 1, 0)
-            + pltpu.roll(density, 1, 1)
-            + pltpu.roll(density, shape[1] - 1, 1)
-        )
-        density = keep * density + gain * beside
-    density_out[...] = density[:BR, :BC]
+        block = step(0, block)
+    for k in range(part):
+        for i in range(2):
+            field[i, pl.ds(k, 8, stride=part), :] = block[k][:, 128 * i : 128 * (i + 1)]
+    for i in range(2):
+        own[:, 128 * i : 128 * (i + 1)] = field[i, :BR]
+    last = pltpu.make_async_copy(own, density_out, sems.at[1])
+    last.start()
+    last.wait()
+    sent.wait()
 
 
 def swap(block, axis, first):
@@ -229,12 +261,25 @@
         [(BR + 16, WIDE), (BR + 16, BC), (BR + 48, 128), (BR + 48, 128)],
         d_own,
         a_own,
+        odd,
         even,
-        odd,
     )
     odd = swap(odd, "col", 1)
     even = swap(even, "col", 0)
-    demand, density = call(final_kernel, [(BR, BC), (BR, BC)], d_ext, a_ext, even, odd)
+    demand, density = pl.pallas_call(
+        final_kernel,
+        out_shape=[jax.ShapeDtypeStruct((BR, BC), F32)] * 2,
+        in_specs=[pl.BlockSpec(memory_space=VMEM)] * 4,
+        out_specs=[pl.BlockSpec(memory_space=HBM)] * 2,
+        scratch_shapes=[
+            pltpu.VMEM((BR, BC), F32),
+            pltpu.VMEM((BR, BC), F32),
+            pltpu.VMEM((3, BR + 16, 128), F32),
+            pltpu.VMEM((3, BR + 16, 128), F32),
+            pltpu.SemaphoreType.DMA((2,)),
+        ],
+        compiler_params=pltpu.CompilerParams(vmem_limit_bytes=40 * 2**20),
+    )(d_ext, a_ext, odd, even)
     return (demand, density)
 
 

time: 29.2 us -> 26.1 us (0.89)
  the two profiles are of different devices: /device:TPU:9 before, /device:TPU:102 now
where the time goes in v3:
time: 26.1 us; the launch traced here: 25.9 us
  starting transfers between devices  14.2 us (54%)
  waiting for transfers between devices  5.5 us (21%)
  Pallas kernels  5.49 us (21%)
  between operations  0.69 us (3%)
    ppermute x4, starting transfers between devices, swap(): lax.ppermute(block, axis, [p for i in pairs for p in ((i, i + 1), (i + 1,...  14.2 us
    ppermute x4, waiting for transfers between devices, swap(): lax.ppermute(block, axis, [p for i in pairs for p in ((i, i + 1), (i + 1,...  5.5 us
    pallas_call x2, Pallas kernels, call(): pl.pallas_call(kernel, out_shape=[jax.ShapeDtypeStruct(s, F32) for s in s...  3.88 us
    pallas_call x1, Pallas kernels, body(): pl.pallas_call(final_kernel, out_shape=[jax.ShapeDtypeStruct((BR, BC), F3...  1.61 us
  transfers between devices with their start and end apart: 4, of which 3 were waited for; matrix products, arithmetic and copies ran while one was open for 0% of the time, Pallas kernels for 0%

profile of v3, /device:TPU:102, one launch (start us, length us, event | category | flops | bytes accessed | tf_op | source)
XLA Modules:
  0.0 25.9 jit_solution(660092280997790876)
XLA Ops:
  0.6 3.7 %shard_map.59 = (f32[136,384]{1,0:T(8,128)S(1)}, f32[128,256]{1,0:T(8,128)S(1)}, f32[80,384]{1,0:T(8,128)S(1)}, f32[80,384]{1,0:T(8,128)S(1)}) custom-call(s32[4,4096]{1,0:T(4,128)} %boxes_in.1, s32[32,128]{1,0:T(8,128)} %bitcast.3, s32[2,16384]{1,0:T(2,128)} %bins_in.1, s32[128,128]{1,0:T(8,128)} %bitcast.2), custom_call_target="tpu_custom_call" | custom-call | tf_op jit(solution)/shard_map/pallas_call | solution.py:233
  4.3 1.9 %collective-permute-start = (f32[80,384]{1,0:T(8,128)S(1)}, f32[80,384]{1,0:T(8,128)S(1)}, u32[]{:S(2)}, u32[]{:S(2)}) collective-permute-start(f32[80,384]{1,0:T(8,128)S(1)} %get-tuple-element.12), channel_id=1, source_target_pairs={{16,32},{32,16},{48,64},{64,48},{80,96},{96,80},{112,128},{128,112... | collective-permute-start | bytes 368648 | tf_op jit(solution)/shard_map/ppermute | solution.py:229
  6.3 5.1 %collective-permute-start.1 = (f32[80,384]{1,0:T(8,128)S(1)}, f32[80,384]{1,0:T(8,128)S(1)}, u32[]{:S(2)}, u32[]{:S(2)}) collective-permute-start(f32[80,384]{1,0:T(8,128)S(1)} %get-tuple-element.13), channel_id=1, source_target_pairs={{0,16},{16,0},{32,48},{48,32},{64,80},{80,64},{96,112},{112,96},{1... | collective-permute-start | bytes 368648 | tf_op jit(solution)/shard_map/ppermute | solution.py:229
  11.4 0.0 collective-permute-done.odd_in
  11.4 0.9 %collective-permute-done.1.even_in = f32[80,384]{1,0:T(8,128)S(1)} collective-permute-done((f32[80,384]{1,0:T(8,128)S(1)}, f32[80,384]{1,0:T(8,128)S(1)}, u32[]{:S(2)}, u32[]{:S(2)}) %collective-permute-start.1) | collective-permute-done | bytes 122912 | tf_op jit(solution)/shard_map/ppermute | solution.py:229
  12.4 0.2 shard_map.60
  12.6 5.2 %collective-permute-start.2 = (f32[176,128]{1,0:T(8,128)S(1)}, f32[176,128]{1,0:T(8,128)S(1)}, u32[]{:S(2)}, u32[]{:S(2)}) collective-permute-start(f32[176,128]{1,0:T(8,128)S(1)} %get-tuple-element.16), channel_id=1, source_target_pairs={{1,2},{2,1},{3,4},{4,3},{5,6},{6,5},{7,8},{8,7},{9,10},{10,9},{11,... | collective-permute-start | bytes 270344 | tf_op jit(solution)/shard_map/ppermute | solution.py:229
  17.8 1.9 %collective-permute-start.3 = (f32[176,128]{1,0:T(8,128)S(1)}, f32[176,128]{1,0:T(8,128)S(1)}, u32[]{:S(2)}, u32[]{:S(2)}) collective-permute-start(f32[176,128]{1,0:T(8,128)S(1)} %get-tuple-element.17), channel_id=1, source_target_pairs={{0,1},{1,0},{2,3},{3,2},{4,5},{5,4},{6,7},{7,6},{8,9},{9,8},{10,11... | collective-permute-start | bytes 270344 | tf_op jit(solution)/shard_map/ppermute | solution.py:229
  19.7 1.7 %collective-permute-done.2.odd_in = f32[176,128]{1,0:T(8,128)S(1)} collective-permute-done((f32[176,128]{1,0:T(8,128)S(1)}, f32[176,128]{1,0:T(8,128)S(1)}, u32[]{:S(2)}, u32[]{:S(2)}) %collective-permute-start.2) | collective-permute-done | bytes 90144 | tf_op jit(solution)/shard_map/ppermute | solution.py:229
  21.4 2.8 %collective-permute-done.3.even_in = f32[176,128]{1,0:T(8,128)S(1)} collective-permute-done((f32[176,128]{1,0:T(8,128)S(1)}, f32[176,128]{1,0:T(8,128)S(1)}, u32[]{:S(2)}, u32[]{:S(2)}) %collective-permute-start.3) | collective-permute-done | bytes 90144 | tf_op jit(solution)/shard_map/ppermute | solution.py:229
  24.2 1.6 %shard_map.61 = (f32[128,256]{1,0:T(8,128)}, f32[128,256]{1,0:T(8,128)}) custom-call(f32[144,384]{1,0:T(8,128)S(1)} %get-tuple-element.14.d_in, f32[144,256]{1,0:T(8,128)S(1)} %get-tuple-element.15.a_in, f32[176,128]{1,0:T(8,128)S(1)} %collective-permute-done.2.odd_in, f32[176,128]{1,0:T(8,128)S(1)} %collective-permute-done.3.even_in), custom_call_target="tpu_custom_call" | custom-call | tf_op jit(solution)/shard_map/pallas_call | solution.py:269
Async XLA Ops:
  4.3 7.1 %collective-permute-start = (f32[80,384]{1,0:T(8,128)S(1)}, f32[80,384]{1,0:T(8,128)S(1)}, u32[]{:S(2)}, u32[]{:S(2)}) collective-permute-start(f32[80,384]{1,0:T(8,128)S(1)} %get-tuple-element.12), channel_id=1, source_target_pairs={{16,32},{32,16},{48,64},{64,48},{80,96},{96,80},{112,128},{128,112... | collective-permute-start | bytes 368648 | tf_op jit(solution)/shard_map/ppermute | solution.py:229
  6.3 6.1 %collective-permute-start.1 = (f32[80,384]{1,0:T(8,128)S(1)}, f32[80,384]{1,0:T(8,128)S(1)}, u32[]{:S(2)}, u32[]{:S(2)}) collective-permute-start(f32[80,384]{1,0:T(8,128)S(1)} %get-tuple-element.13), channel_id=1, source_target_pairs={{0,16},{16,0},{32,48},{48,32},{64,80},{80,64},{96,112},{112,96},{1... | collective-permute-start | bytes 368648 | tf_op jit(solution)/shard_map/ppermute | solution.py:229
  12.6 8.9 %collective-permute-start.2 = (f32[176,128]{1,0:T(8,128)S(1)}, f32[176,128]{1,0:T(8,128)S(1)}, u32[]{:S(2)}, u32[]{:S(2)}) collective-permute-start(f32[176,128]{1,0:T(8,128)S(1)} %get-tuple-element.16), channel_id=1, source_target_pairs={{1,2},{2,1},{3,4},{4,3},{5,6},{6,5},{7,8},{8,7},{9,10},{10,9},{11,... | collective-permute-start | bytes 270344 | tf_op jit(solution)/shard_map/ppermute | solution.py:229
  17.8 6.5 %collective-permute-start.3 = (f32[176,128]{1,0:T(8,128)S(1)}, f32[176,128]{1,0:T(8,128)S(1)}, u32[]{:S(2)}, u32[]{:S(2)}) collective-permute-start(f32[176,128]{1,0:T(8,128)S(1)} %get-tuple-element.17), channel_id=1, source_target_pairs={{0,1},{1,0},{2,3},{3,2},{4,5},{5,4},{6,7},{7,6},{8,9},{9,8},{10,11... | collective-permute-start | bytes 270344 | tf_op jit(solution)/shard_map/ppermute | solution.py:229

commit v4 on v3

--- a/solution.py
+++ b/solution.py
@@ -8,6 +8,7 @@
 BR = 128
 BC = 256
 STEPS = 6
+PART = (BR + 16) // 8
 TALL = 192
 WIDE = 384
 NET_BLOCK = 4096
@@ -85,7 +86,7 @@
     zero = jnp.zeros((), BF16)
 
     def add_nets(i, demand):
-        k = pl.multiple_of(i * n, n)
+        k = i * n
         box = boxes[:, pl.ds(k, n)]
         y0, y1, x0, x1 = (box[i : i + 1] for i in range(4))
         top = y0 & (BR - 1)
@@ -102,7 +103,7 @@
         right = jnp.where(inside, repeated(lane_row(col_factor, k, n), 16, BF16), zero)
         return demand + nt_dot(right.reshape(WIDE, n), down.reshape(TALL, n))
 
-    demand = lax.fori_loop(0, boxes.shape[1] // n, add_nets, jnp.zeros((WIDE, TALL), F32))
+    demand = add_nets(0, jnp.zeros((WIDE, TALL), F32))
     copies[2].wait()
     copies[3].wait()
     m = CELL_BLOCK
@@ -125,11 +126,11 @@
             (where[1:2] & (BC - 1)) - 128, 32, jnp.int8
         )
         right = jnp.where(cols, one, zero).reshape(BC, m)
-        return total + nt_dot(right, down)
-
-    total = lax.fori_loop(0, bins.shape[1] // m, add_cells, jnp.zeros((BC, 2 * BR), F32))
+        return total + nt_dot(down, right)
+
+    total = lax.fori_loop(0, bins.shape[1] // m, add_cells, jnp.zeros((2 * BR, BC), F32))
     demand = demand.T
-    total = (total[:, :BR] * 0.5 + total[:, BR:] * (1.0 / 16.0)).T
+    total = total[:BR] * 0.5 + total[BR:] * (1.0 / 16.0)
     d_out[...] = demand[: BR + 8]
     a_out[...] = total
     even = lax.rem(lax.axis_index("row"), 2) == 0
@@ -140,7 +141,7 @@
         message[72:, :BC] = jnp.where(goes_down, total[BR - 8 :], total[:8])
 
 
-def merge_kernel(d_own, a_own, odd_in, even_in, d_out, a_out, even_out, odd_out):
+def merge_kernel(d_own, a_own, odd_in, even_in, d_out, a_out, right_out, left_out):
     even = lax.rem(lax.axis_index("row"), 2) == 0
     above = jnp.where(even, odd_in[...], even_in[...])
     below = jnp.where(even, even_in[:8], odd_in[:8])
@@ -152,81 +153,124 @@
     d_out[...] = demand
     a_out[...] = area
     lane = lax.broadcasted_iota(jnp.int32, (BR + 16, 128), 1)
-    leftward = jnp.where(lane < 8, demand[:, :128], pltpu.roll(area[:, :128], 8, 1))
+    first = jnp.where(lane < 8, demand[:, :128], pltpu.roll(area[:, :128], 8, 1))
     strip = jnp.where(lane < 120, pltpu.roll(demand[:, 128:BC], 120, 1), area[:, 128:])
-    strip = jnp.concatenate([strip, jnp.zeros((112, 128), F32)], axis=0).T[112:]
-    even = lax.rem(lax.axis_index("col"), 2) == 0
-    for message, goes_right in ((even_out, even), (odd_out, jnp.logical_not(even))):
-        message[: BR + 16] = jnp.where(goes_right, demand[:, BC:], leftward)
-        message[BR + 16 : BR + 32] = strip[:, :128]
-        message[BR + 32 :] = strip[:, 128:]
+    strip = jnp.where(lane < 16, first, strip)
+    strip = jnp.concatenate([strip, jnp.zeros((112, 128), F32)], axis=0).T
+    right_out[: BR + 16] = demand[:, BC:]
+    right_out[BR + 16 : BR + 32] = strip[112:, :128]
+    right_out[BR + 32 :] = strip[112:, 128:]
+    left_out[:16] = strip[:16, :128]
+    left_out[16:] = strip[:16, 128:]
+
+
+def inside_of(col):
+    row = lax.broadcasted_iota(jnp.int32, col.shape, 0)
+    row = jnp.where(row < BR + 8, row, row - (BR + 16)) + lax.axis_index("row") * BR
+    col = col + lax.axis_index("col") * BC
+    rows, cols = lax.axis_size("row") * BR, lax.axis_size("col") * BC
+    inside = (row >= 0) & (row < rows) & (col >= 0) & (col < cols)
+    return jnp.where(inside, 1.0, 0.0)
+
+
+def inflated(demand, area):
+    return (1.0 + 1.5 * demand / (1.0 + demand)) * area
+
+
+def blocks_of(value, field):
+    for i in range(2):
+        field[i] = value[:, 128 * i : 128 * (i + 1)]
+    return [
+        jnp.concatenate([field[i, pl.ds(k, 8, stride=PART), :] for i in range(2)], axis=1)
+        for k in range(PART)
+    ]
+
+
+def diffused(block, inner):
+    for _ in range(STEPS):
+        rows = [pltpu.roll(block[-1], 1, 0), *block, pltpu.roll(block[0], 7, 0)]
+        block = []
+        for k in range(PART):
+            mid = rows[k + 1]
+            beside = rows[k] + rows[k + 2] + pltpu.roll(mid, 1, 1) + pltpu.roll(mid, 255, 1)
+            block.append(inner(k) * (0.04 * mid + 0.24 * beside))
+    return block
+
+
+def half_kernel(d_in, a_in, spread_out, mask_out, field):
+    lane = lax.broadcasted_iota(jnp.int32, (BR + 16, BC), 1)
+    col = jnp.where(lane < 160, lane, jnp.where(lane < 224, lane + 64, lane - BC))
+    for k, block in enumerate(blocks_of(inside_of(col), field)):
+        mask_out[8 * k : 8 * k + 8] = block
+    mask = inside_of(jnp.where(lane < 64, lane + BC, lane))
+    mask = blocks_of(mask, field)
+    start = inflated(d_in[:, 128:BC], a_in[:, 128:]) * inside_of(lane[:, 128:])
+    start = jnp.concatenate([jnp.zeros((BR + 16, 128), F32), start], axis=1)
+    block = diffused(blocks_of(start, field), lambda k: mask[k])
+    for k in range(PART):
+        spread_out[8 * k : 8 * k + 8] = jnp.where(lane[:8] < 64, 0.0, block[k])
 
 
 def final_kernel(
-    d_in, a_in, odd_in, even_in, demand_out, density_out, whole, own, field, inner, sems
+    d_in, a_in, half, mask, left, right, demand_out, density_out, own, field, sems
 ):
     tall = BR + 16
-    even = lax.rem(lax.axis_index("col"), 2) == 0
-    left = jnp.where(even, odd_in[...], even_in[...])
-    right = jnp.where(even, even_in[:tall], odd_in[:tall])
-    strip = jnp.concatenate([left[tall : tall + 16], left[tall + 16 :]], axis=1)
-    strip = jnp.concatenate([jnp.zeros((112, 256), F32), strip], axis=0).T[:tall]
+    strip = jnp.concatenate(
+        [
+            jnp.concatenate([right[:16], right[16:]], axis=1),
+            jnp.zeros((96, 256), F32),
+            jnp.concatenate([left[tall : tall + 16], left[tall + 16 :]], axis=1),
+        ],
+        axis=0,
+    ).T[:tall]
+    low = d_in[:, :128] + left[:tall]
+    own[...] = low[:BR]
+    copies = [
+        pltpu.make_async_copy(own, demand_out.at[:, :128], sems.at[0]),
+        pltpu.make_async_copy(d_in.at[:BR, 128:BC], demand_out.at[:, 128:], sems.at[1]),
+    ]
+    for copy in copies:
+        copy.start()
     lane = lax.broadcasted_iota(jnp.int32, (tall, 128), 1)
-    beyond = jnp.where(lane < 8, d_in[:, BC:] + right, pltpu.roll(strip, 8, 1))
-    demand = jnp.concatenate([d_in[:, :128] + left[:tall], d_in[:, 128:BC], beyond], axis=1)
-    beyond = jnp.where(lane < 8, pltpu.roll(right, 120, 1), strip)
-    area = jnp.concatenate([a_in[...], beyond], axis=1)
-    whole[...] = demand[:BR, :BC]
-    sent = pltpu.make_async_copy(whole, demand_out, sems.at[0])
-    sent.start()
-    shape = demand.shape
-    row = lax.broadcasted_iota(jnp.int32, shape, 0)
-    row = jnp.where(row < BR + 8, row, row - tall) + lax.axis_index("row") * BR
-    lane = lax.broadcasted_iota(jnp.int32, shape, 1)
-    near = (lane < BC + 8) | (lane >= WIDE - 8)
-    col = jnp.where(lane < BC + 8, lane, lane - WIDE) + lax.axis_index("col") * BC
-    rows, cols = lax.axis_size("row") * BR, lax.axis_size("col") * BC
-    inside = near & (row >= 0) & (row < rows) & (col >= 0) & (col < cols)
-    start = (1.0 + 1.5 * demand / (1.0 + demand)) * area
-    density = jnp.where(inside, start, 0.0)
-    mask = jnp.where(inside, 1.0, 0.0)
-    for i in range(3):
-        field[i] = density[:, 128 * i : 128 * (i + 1)]
-        inner[i] = mask[:, 128 * i : 128 * (i + 1)]
-    part = shape[0] // 8
-
-    def strided(ref, k):
-        return jnp.concatenate([ref[i, pl.ds(k, 8, stride=part), :] for i in range(3)], axis=1)
-
-    block = [strided(field, k) for k in range(part)]
-
-    def step(_, block):
-        first = pltpu.roll(block[-1], 1, 0)
-        last = pltpu.roll(block[0], 7, 0)
-        rows = [first, *block, last]
-        new = []
-        for k in range(part):
-            mid = rows[k + 1]
-            beside = rows[k] + rows[k + 2] + pltpu.roll(mid, 1, 1) + pltpu.roll(mid, WIDE - 1, 1)
-            new.append(strided(inner, k) * (0.04 * mid + 0.24 * beside))
-        return tuple(new)
-
-    for _ in range(STEPS):
-        block = step(0, block)
-    for k in range(part):
-        for i in range(2):
-            field[i, pl.ds(k, 8, stride=part), :] = block[k][:, 128 * i : 128 * (i + 1)]
+    demand = pltpu.roll(jnp.where(lane < 8, d_in[:, BC:] + strip, 0.0), 64, 1)
+    demand = jnp.where(lane < 120, demand, pltpu.roll(strip, 8, 1))
+    used = ((lane >= 64) & (lane < 72)) | (lane >= 120)
+    area = jnp.where(lane < 120, pltpu.roll(strip, 56, 1), strip)
+    start = inflated(demand, jnp.where(used, area, 0.0))
+    start = jnp.concatenate([inflated(low, a_in[:, :128]), start], axis=1)
+    block = blocks_of(start, field)
+
+    def inner(k):
+        return mask[8 * k : 8 * k + 8]
+
+    block = diffused([inner(k) * block[k] for k in range(PART)], inner)
+    lane = lane[:8]
+    for k in range(PART):
+        known = half[8 * k : 8 * k + 8]
+        field[0, pl.ds(k, 8, stride=PART), :] = block[k][:, :128] + known[:, :128]
+        more = block[k][:, 128:]
+        more = jnp.where(lane < 32, more, jnp.where(lane >= 96, pltpu.roll(more, 64, 1), 0.0))
+        field[1, pl.ds(k, 8, stride=PART), :] = more + known[:, 128:]
     for i in range(2):
-        own[:, 128 * i : 128 * (i + 1)] = field[i, :BR]
-    last = pltpu.make_async_copy(own, density_out, sems.at[1])
-    last.start()
-    last.wait()
-    sent.wait()
+        copies.append(
+            pltpu.make_async_copy(
+                field.at[i, :BR], density_out.at[:, 128 * i : 128 * (i + 1)], sems.at[2 + i]
+            )
+        )
+        copies[-1].start()
+    for copy in copies:
+        copy.wait()
 
 
 def swap(block, axis, first):
     pairs = range(first, lax.axis_size(axis) - 1, 2)
     return lax.ppermute(block, axis, [p for i in pairs for p in ((i, i + 1), (i + 1, i))])
+
+
+def shift(block, axis, distance):
+    devices = range(lax.axis_size(axis))
+    route = [(i, i + distance) for i in devices if i + distance in devices]
+    return lax.ppermute(block, axis, route)
 
 
 def call(kernel, shapes, *args, space=VMEM, scratch=()):
@@ -256,30 +300,34 @@
     )
     odd = swap(odd, "row", 1)
     even = swap(even, "row", 0)
-    d_ext, a_ext, even, odd = call(
+    d_ext, a_ext, right, left = call(
         merge_kernel,
-        [(BR + 16, WIDE), (BR + 16, BC), (BR + 48, 128), (BR + 48, 128)],
+        [(BR + 16, WIDE), (BR + 16, BC), (BR + 48, 128), (32, 128)],
         d_own,
         a_own,
         odd,
         even,
     )
-    odd = swap(odd, "col", 1)
-    even = swap(even, "col", 0)
+    left, right = shift(right, "col", 1), shift(left, "col", -1)
+    half, mask = call(
+        half_kernel,
+        [(BR + 16, BC), (BR + 16, BC)],
+        d_ext,
+        a_ext,
+        scratch=[pltpu.VMEM((2, BR + 16, 128), F32)],
+    )
     demand, density = pl.pallas_call(
         final_kernel,
         out_shape=[jax.ShapeDtypeStruct((BR, BC), F32)] * 2,
-        in_specs=[pl.BlockSpec(memory_space=VMEM)] * 4,
+        in_specs=[pl.BlockSpec(memory_space=VMEM)] * 6,
         out_specs=[pl.BlockSpec(memory_space=HBM)] * 2,
         scratch_shapes=[
-            pltpu.VMEM((BR, BC), F32),
-            pltpu.VMEM((BR, BC), F32),
-            pltpu.VMEM((3, BR + 16, 128), F32),
-            pltpu.VMEM((3, BR + 16, 128), F32),
-            pltpu.SemaphoreType.DMA((2,)),
+            pltpu.VMEM((BR, 128), F32),
+            pltpu.VMEM((2, BR + 16, 128), F32),
+            pltpu.SemaphoreType.DMA((4,)),
         ],
         compiler_params=pltpu.CompilerParams(vmem_limit_bytes=40 * 2**20),
-    )(d_ext, a_ext, odd, even)
+    )(d_ext, a_ext, half, mask, left, right)
     return (demand, density)
 
 

time: 26.1 us -> 25.1 us (0.962)
  the two profiles are of different devices: /device:TPU:102 before, /device:TPU:122 now
where the time goes in v4:
time: 25.1 us; the launch traced here: 24.9 us
  starting transfers between devices  12.9 us (51%)
  Pallas kernels  6 us (24%)
  waiting for transfers between devices  5.25 us (21%)
  between operations  0.69 us (3%)
    ppermute x2, starting transfers between devices, swap(): lax.ppermute(block, axis, [p for i in pairs for p in ((i, i + 1), (i + 1,...  7.06 us
    ppermute x2, starting transfers between devices, shift(): return lax.ppermute(block, axis, route)  5.86 us
    pallas_call x3, Pallas kernels, call(): pl.pallas_call(kernel, out_shape=[jax.ShapeDtypeStruct(s, F32) for s in s...  4.49 us
    ppermute x2, waiting for transfers between devices, shift(): return lax.ppermute(block, axis, route)  4.3 us
    pallas_call x1, Pallas kernels, body(): pl.pallas_call(final_kernel, out_shape=[jax.ShapeDtypeStruct((BR, BC), F3...  1.51 us
    ppermute x2, waiting for transfers between devices, swap(): lax.ppermute(block, axis, [p for i in pairs for p in ((i, i + 1), (i + 1,...  0.95 us
  transfers between devices with their start and end apart: 4, of which 2 were waited for; matrix products, arithmetic and copies ran while one was open for 0% of the time, Pallas kernels for 3%

profile of v4, /device:TPU:122, one launch (start us, length us, event | category | flops | bytes accessed | tf_op | source)
XLA Modules:
  0.0 24.9 jit_solution(25012117075155222)
XLA Ops:
  0.6 3.7 %shard_map.59 = (f32[136,384]{1,0:T(8,128)S(1)}, f32[128,256]{1,0:T(8,128)S(1)}, f32[80,384]{1,0:T(8,128)S(1)}, f32[80,384]{1,0:T(8,128)S(1)}) custom-call(s32[4,4096]{1,0:T(4,128)} %boxes_in.1, s32[32,128]{1,0:T(8,128)} %bitcast.3, s32[2,16384]{1,0:T(2,128)} %bins_in.1, s32[128,128]{1,0:T(8,128)} %bitcast.2), custom_call_target="tpu_custom_call" | custom-call | tf_op jit(solution)/shard_map/pallas_call | solution.py:277
  4.3 1.9 %collective-permute-start = (f32[80,384]{1,0:T(8,128)S(1)}, f32[80,384]{1,0:T(8,128)S(1)}, u32[]{:S(2)}, u32[]{:S(2)}) collective-permute-start(f32[80,384]{1,0:T(8,128)S(1)} %get-tuple-element.14), channel_id=1, source_target_pairs={{16,32},{32,16},{48,64},{64,48},{80,96},{96,80},{112,128},{128,112... | collective-permute-start | bytes 368648 | tf_op jit(solution)/shard_map/ppermute | solution.py:267
  6.2 5.1 %collective-permute-start.1 = (f32[80,384]{1,0:T(8,128)S(1)}, f32[80,384]{1,0:T(8,128)S(1)}, u32[]{:S(2)}, u32[]{:S(2)}) collective-permute-start(f32[80,384]{1,0:T(8,128)S(1)} %get-tuple-element.15), channel_id=1, source_target_pairs={{0,16},{16,0},{32,48},{48,32},{64,80},{80,64},{96,112},{112,96},{1... | collective-permute-start | bytes 368648 | tf_op jit(solution)/shard_map/ppermute | solution.py:267
  11.4 0.0 collective-permute-done.odd_in
  11.4 0.9 %collective-permute-done.1.even_in = f32[80,384]{1,0:T(8,128)S(1)} collective-permute-done((f32[80,384]{1,0:T(8,128)S(1)}, f32[80,384]{1,0:T(8,128)S(1)}, u32[]{:S(2)}, u32[]{:S(2)}) %collective-permute-start.1) | collective-permute-done | bytes 122912 | tf_op jit(solution)/shard_map/ppermute | solution.py:267
  12.3 0.2 shard_map.60
  12.5 3.1 %collective-permute-start.2 = (f32[176,128]{1,0:T(8,128)S(1)}, f32[176,128]{1,0:T(8,128)S(1)}, u32[]{:S(2)}, u32[]{:S(2)}) collective-permute-start(f32[176,128]{1,0:T(8,128)S(1)} %get-tuple-element.20), channel_id=1, source_target_pairs={{0,1},{1,2},{2,3},{3,4},{4,5},{5,6},{6,7},{7,8},{8,9},{9,10},{10,1... | collective-permute-start | bytes 270344 | tf_op jit(solution)/shard_map/ppermute | solution.py:273
  15.6 2.8 %collective-permute-start.3 = (f32[32,128]{1,0:T(8,128)S(1)}, f32[32,128]{1,0:T(8,128)S(1)}, u32[]{:S(2)}, u32[]{:S(2)}) collective-permute-start(f32[32,128]{1,0:T(8,128)S(1)} %get-tuple-element.21), channel_id=1, source_target_pairs={{1,0},{2,1},{3,2},{4,3},{5,4},{6,5},{7,6},{8,7},{9,8},{10,9},{11,1... | collective-permute-start | bytes 49160 | tf_op jit(solution)/shard_map/ppermute | solution.py:273
  18.4 0.6 %shard_map.61 = (f32[144,256]{1,0:T(8,128)S(1)}, f32[144,256]{1,0:T(8,128)S(1)}) custom-call(f32[144,384]{1,0:T(8,128)S(1)} %get-tuple-element.16.d_in, f32[144,256]{1,0:T(8,128)S(1)} %get-tuple-element.17.a_in), custom_call_target="tpu_custom_call" | custom-call | tf_op jit(solution)/shard_map/pallas_call | solution.py:277
  19.1 4.3 %collective-permute-done.3.right = f32[32,128]{1,0:T(8,128)S(1)} collective-permute-done((f32[32,128]{1,0:T(8,128)S(1)}, f32[32,128]{1,0:T(8,128)S(1)}, u32[]{:S(2)}, u32[]{:S(2)}) %collective-permute-start.3) | collective-permute-done | bytes 16416 | tf_op jit(solution)/shard_map/ppermute | solution.py:273
  23.4 0.0 collective-permute-done.2.left
  23.4 1.5 %shard_map.62 = (f32[128,256]{1,0:T(8,128)}, f32[128,256]{1,0:T(8,128)}) custom-call(f32[144,384]{1,0:T(8,128)S(1)} %get-tuple-element.16.d_in, f32[144,256]{1,0:T(8,128)S(1)} %get-tuple-element.17.a_in, f32[144,256]{1,0:T(8,128)S(1)} %get-tuple-element.18.half, f32[144,256]{1,0:T(8,128)S(1)} %get-tuple-element.19.mask, ...), custom_call_target="tpu_custom_call" | custom-call | tf_op jit(solution)/shard_map/pallas_call | solution.py:319
Async XLA Ops:
  4.3 7.1 %collective-permute-start = (f32[80,384]{1,0:T(8,128)S(1)}, f32[80,384]{1,0:T(8,128)S(1)}, u32[]{:S(2)}, u32[]{:S(2)}) collective-permute-start(f32[80,384]{1,0:T(8,128)S(1)} %get-tuple-element.14), channel_id=1, source_target_pairs={{16,32},{32,16},{48,64},{64,48},{80,96},{96,80},{112,128},{128,112... | collective-permute-start | bytes 368648 | tf_op jit(solution)/shard_map/ppermute | solution.py:267
  6.2 6.1 %collective-permute-start.1 = (f32[80,384]{1,0:T(8,128)S(1)}, f32[80,384]{1,0:T(8,128)S(1)}, u32[]{:S(2)}, u32[]{:S(2)}) collective-permute-start(f32[80,384]{1,0:T(8,128)S(1)} %get-tuple-element.15), channel_id=1, source_target_pairs={{0,16},{16,0},{32,48},{48,32},{64,80},{80,64},{96,112},{112,96},{1... | collective-permute-start | bytes 368648 | tf_op jit(solution)/shard_map/ppermute | solution.py:267
  12.5 10.8 %collective-permute-start.2 = (f32[176,128]{1,0:T(8,128)S(1)}, f32[176,128]{1,0:T(8,128)S(1)}, u32[]{:S(2)}, u32[]{:S(2)}) collective-permute-start(f32[176,128]{1,0:T(8,128)S(1)} %get-tuple-element.20), channel_id=1, source_target_pairs={{0,1},{1,2},{2,3},{3,4},{4,5},{5,6},{6,7},{7,8},{8,9},{9,10},{10,1... | collective-permute-start | bytes 270344 | tf_op jit(solution)/shard_map/ppermute | solution.py:273
  15.6 7.7 %collective-permute-start.3 = (f32[32,128]{1,0:T(8,128)S(1)}, f32[32,128]{1,0:T(8,128)S(1)}, u32[]{:S(2)}, u32[]{:S(2)}) collective-permute-start(f32[32,128]{1,0:T(8,128)S(1)} %get-tuple-element.21), channel_id=1, source_target_pairs={{1,0},{2,1},{3,2},{4,3},{5,4},{6,5},{7,6},{8,7},{9,8},{10,9},{11,1... | collective-permute-start | bytes 49160 | tf_op jit(solution)/shard_map/ppermute | solution.py:273

commit v5 on v4

--- a/solution.py
+++ b/solution.py
@@ -141,6 +141,11 @@
         message[72:, :BC] = jnp.where(goes_down, total[BR - 8 :], total[:8])
 
 
+def lying(strip):
+    gap = jnp.zeros((112, 128), F32)
+    return jnp.concatenate([strip[: BR + 8], gap, strip[BR + 8 :]], axis=0).T
+
+
 def merge_kernel(d_own, a_own, odd_in, even_in, d_out, a_out, right_out, left_out):
     even = lax.rem(lax.axis_index("row"), 2) == 0
     above = jnp.where(even, odd_in[...], even_in[...])
@@ -156,7 +161,7 @@
     first = jnp.where(lane < 8, demand[:, :128], pltpu.roll(area[:, :128], 8, 1))
     strip = jnp.where(lane < 120, pltpu.roll(demand[:, 128:BC], 120, 1), area[:, 128:])
     strip = jnp.where(lane < 16, first, strip)
-    strip = jnp.concatenate([strip, jnp.zeros((112, 128), F32)], axis=0).T
+    strip = lying(strip)
     right_out[: BR + 16] = demand[:, BC:]
     right_out[BR + 16 : BR + 32] = strip[112:, :128]
     right_out[BR + 32 :] = strip[112:, 128:]
@@ -178,32 +183,39 @@
 
 
 def blocks_of(value, field):
-    for i in range(2):
+    tiles = range(value.shape[1] // 128)
+    for i in tiles:
         field[i] = value[:, 128 * i : 128 * (i + 1)]
     return [
-        jnp.concatenate([field[i, pl.ds(k, 8, stride=PART), :] for i in range(2)], axis=1)
+        jnp.concatenate([field[i, pl.ds(k, 8, stride=PART), :] for i in tiles], axis=1)
         for k in range(PART)
     ]
 
 
 def diffused(block, inner):
+    wide = block[0].shape[1]
     for _ in range(STEPS):
         rows = [pltpu.roll(block[-1], 1, 0), *block, pltpu.roll(block[0], 7, 0)]
         block = []
         for k in range(PART):
             mid = rows[k + 1]
-            beside = rows[k] + rows[k + 2] + pltpu.roll(mid, 1, 1) + pltpu.roll(mid, 255, 1)
+            beside = rows[k] + rows[k + 2] + pltpu.roll(mid, 1, 1) + pltpu.roll(mid, wide - 1, 1)
             block.append(inner(k) * (0.04 * mid + 0.24 * beside))
     return block
 
 
-def half_kernel(d_in, a_in, spread_out, mask_out, field):
+def upright(strip):
+    strip = jnp.concatenate([strip[:16], strip[16:]], axis=1)
+    strip = jnp.concatenate([jnp.zeros((112, 256), F32), strip], axis=0).T
+    return jnp.concatenate([strip[: BR + 8], strip[248:]], axis=0)
+
+
+def middle_kernel(d_in, a_in, spread_out, mask_out, over_out, field):
     lane = lax.broadcasted_iota(jnp.int32, (BR + 16, BC), 1)
-    col = jnp.where(lane < 160, lane, jnp.where(lane < 224, lane + 64, lane - BC))
-    for k, block in enumerate(blocks_of(inside_of(col), field)):
+    for k, block in enumerate(blocks_of(inside_of(jnp.where(lane < 192, lane, lane - BC)), field)):
         mask_out[8 * k : 8 * k + 8] = block
-    mask = inside_of(jnp.where(lane < 64, lane + BC, lane))
-    mask = blocks_of(mask, field)
+    over_out[...] = lying(d_in[:, BC:])[:8]
+    mask = blocks_of(inside_of(jnp.where(lane < 64, lane + BC, lane)), field)
     start = inflated(d_in[:, 128:BC], a_in[:, 128:]) * inside_of(lane[:, 128:])
     start = jnp.concatenate([jnp.zeros((BR + 16, 128), F32), start], axis=1)
     block = diffused(blocks_of(start, field), lambda k: mask[k])
@@ -211,18 +223,8 @@
         spread_out[8 * k : 8 * k + 8] = jnp.where(lane[:8] < 64, 0.0, block[k])
 
 
-def final_kernel(
-    d_in, a_in, half, mask, left, right, demand_out, density_out, own, field, sems
-):
+def low_kernel(d_in, a_in, spread, mask, left, demand_out, spread_out, own, field, sems):
     tall = BR + 16
-    strip = jnp.concatenate(
-        [
-            jnp.concatenate([right[:16], right[16:]], axis=1),
-            jnp.zeros((96, 256), F32),
-            jnp.concatenate([left[tall : tall + 16], left[tall + 16 :]], axis=1),
-        ],
-        axis=0,
-    ).T[:tall]
     low = d_in[:, :128] + left[:tall]
     own[...] = low[:BR]
     copies = [
@@ -231,12 +233,9 @@
     ]
     for copy in copies:
         copy.start()
+    strip = upright(left[tall:])
     lane = lax.broadcasted_iota(jnp.int32, (tall, 128), 1)
-    demand = pltpu.roll(jnp.where(lane < 8, d_in[:, BC:] + strip, 0.0), 64, 1)
-    demand = jnp.where(lane < 120, demand, pltpu.roll(strip, 8, 1))
-    used = ((lane >= 64) & (lane < 72)) | (lane >= 120)
-    area = jnp.where(lane < 120, pltpu.roll(strip, 56, 1), strip)
-    start = inflated(demand, jnp.where(used, area, 0.0))
+    start = jnp.where(lane >= 120, inflated(pltpu.roll(strip, 8, 1), strip), 0.0)
     start = jnp.concatenate([inflated(low, a_in[:, :128]), start], axis=1)
     block = blocks_of(start, field)
 
@@ -244,22 +243,44 @@
         return mask[8 * k : 8 * k + 8]
 
     block = diffused([inner(k) * block[k] for k in range(PART)], inner)
-    lane = lane[:8]
+    lane = lax.broadcasted_iota(jnp.int32, (8, BC), 1)
     for k in range(PART):
-        known = half[8 * k : 8 * k + 8]
-        field[0, pl.ds(k, 8, stride=PART), :] = block[k][:, :128] + known[:, :128]
-        more = block[k][:, 128:]
-        more = jnp.where(lane < 32, more, jnp.where(lane >= 96, pltpu.roll(more, 64, 1), 0.0))
-        field[1, pl.ds(k, 8, stride=PART), :] = more + known[:, 128:]
-    for i in range(2):
-        copies.append(
-            pltpu.make_async_copy(
-                field.at[i, :BR], density_out.at[:, 128 * i : 128 * (i + 1)], sems.at[2 + i]
-            )
-        )
-        copies[-1].start()
+        known = jnp.where(lane < 192, block[k], 0.0) + spread[8 * k : 8 * k + 8]
+        for i in range(2):
+            part = known[:, 128 * i : 128 * (i + 1)]
+            spread_out[i, pl.ds(k, 8, stride=PART), :] = part
     for copy in copies:
         copy.wait()
+
+
+def edge_kernel(spread, over, right, density_out, own, sems):
+    first = pltpu.make_async_copy(spread.at[0, :BR], density_out.at[:, :128], sems.at[0])
+    first.start()
+    strip = jnp.concatenate([right[:16], right[16:]], axis=1)
+    start = inflated(strip[:8] + over[...], strip[8:])
+    none = jnp.zeros((8, 256), F32)
+    density = jnp.concatenate([none, start, none], axis=0)
+    tall, wide = density.shape
+    col = lax.broadcasted_iota(jnp.int32, (tall, wide), 0) + 248 + lax.axis_index("col") * BC
+    row = lax.broadcasted_iota(jnp.int32, (tall, wide), 1)
+    row = jnp.where(row < 192, row, row - wide) + lax.axis_index("row") * BR
+    inside = (row >= 0) & (row < lax.axis_size("row") * BR) & (col < lax.axis_size("col") * BC)
+    inside = jnp.where(inside, 1.0, 0.0)
+    density = density * inside
+    for _ in range(STEPS):
+        beside = (
+            pltpu.roll(density, 1, 0)
+            + pltpu.roll(density, tall - 1, 0)
+            + pltpu.roll(density, 1, 1)
+            + pltpu.roll(density, wide - 1, 1)
+        )
+        density = inside * (0.04 * density + 0.24 * beside)
+    share = jnp.concatenate([jnp.zeros((120, 128), F32), density[:8, :128]], axis=0).T
+    own[...] = spread[1, :BR] + share
+    last = pltpu.make_async_copy(own, density_out.at[:, 128:], sems.at[1])
+    last.start()
+    first.wait()
+    last.wait()
 
 
 def swap(block, axis, first):
@@ -273,12 +294,12 @@
     return lax.ppermute(block, axis, route)
 
 
-def call(kernel, shapes, *args, space=VMEM, scratch=()):
+def call(kernel, shapes, *args, space=VMEM, outs=None, scratch=()):
     return pl.pallas_call(
         kernel,
         out_shape=[jax.ShapeDtypeStruct(s, F32) for s in shapes],
         in_specs=[pl.BlockSpec(memory_space=space)] * len(args),
-        out_specs=[pl.BlockSpec(memory_space=VMEM)] * len(shapes),
+        out_specs=[pl.BlockSpec(memory_space=s) for s in outs or [VMEM] * len(shapes)],
         scratch_shapes=list(scratch),
         compiler_params=pltpu.CompilerParams(vmem_limit_bytes=40 * 2**20),
     )(*args)
@@ -309,25 +330,36 @@
         even,
     )
     left, right = shift(right, "col", 1), shift(left, "col", -1)
-    half, mask = call(
-        half_kernel,
-        [(BR + 16, BC), (BR + 16, BC)],
+    tall = BR + 16
+    field = pltpu.VMEM((2, tall, 128), F32)
+    two = pltpu.SemaphoreType.DMA((2,))
+    spread, mask, over = call(
+        middle_kernel,
+        [(tall, BC), (tall, BC), (8, 256)],
         d_ext,
         a_ext,
-        scratch=[pltpu.VMEM((2, BR + 16, 128), F32)],
-    )
-    demand, density = pl.pallas_call(
-        final_kernel,
-        out_shape=[jax.ShapeDtypeStruct((BR, BC), F32)] * 2,
-        in_specs=[pl.BlockSpec(memory_space=VMEM)] * 6,
-        out_specs=[pl.BlockSpec(memory_space=HBM)] * 2,
-        scratch_shapes=[
-            pltpu.VMEM((BR, 128), F32),
-            pltpu.VMEM((2, BR + 16, 128), F32),
-            pltpu.SemaphoreType.DMA((4,)),
-        ],
-        compiler_params=pltpu.CompilerParams(vmem_limit_bytes=40 * 2**20),
-    )(d_ext, a_ext, half, mask, left, right)
+        scratch=[field],
+    )
+    demand, spread = call(
+        low_kernel,
+        [(BR, BC), (2, tall, 128)],
+        d_ext,
+        a_ext,
+        spread,
+        mask,
+        left,
+        outs=[HBM, VMEM],
+        scratch=[pltpu.VMEM((BR, 128), F32), field, two],
+    )
+    (density,) = call(
+        edge_kernel,
+        [(BR, BC)],
+        spread,
+        over,
+        right,
+        outs=[HBM],
+        scratch=[pltpu.VMEM((BR, 128), F32), two],
+    )
     return (demand, density)
 
 

time: 25.1 us -> 24.7 us (0.984)
  waiting for transfers between devices: 5.25 us -> 3.95 us
  Pallas kernels: 6 us -> 6.93 us
    pallas_call x3 -> x5, Pallas kernels: 4.49 us -> 6.93 us  [call(): pl.pallas_call(kernel, out_shape=[jax.ShapeDtypeStruct(s, F32) for s in s...]
    pallas_call x1 -> x0, Pallas kernels: 1.51 us -> none  [body(): pl.pallas_call(final_kernel, out_shape=[jax.ShapeDtypeStruct((BR, BC), F3...]
    ppermute x2, waiting for transfers between devices: 4.3 us -> 3 us  [shift(): return lax.ppermute(block, axis, route)]
  transfers between devices with their start and end apart: 4 -> 4, of which waited for: 2 -> 3; matrix products, arithmetic and copies ran while one was open for 0% -> 0% of each run, Pallas kernels for 3% -> 8%
where the time goes in v5:
time: 24.7 us; the launch traced here: 24.5 us
  starting transfers between devices  12.9 us (52%)
  Pallas kernels  6.93 us (28%)
  waiting for transfers between devices  3.95 us (16%)
  between operations  0.7 us (3%)
    ppermute x2, starting transfers between devices, swap(): lax.ppermute(block, axis, [p for i in pairs for p in ((i, i + 1), (i + 1,...  7.06 us
    pallas_call x5, Pallas kernels, call(): pl.pallas_call(kernel, out_shape=[jax.ShapeDtypeStruct(s, F32) for s in s...  6.93 us
    ppermute x2, starting transfers between devices, shift(): return lax.ppermute(block, axis, route)  5.86 us
    ppermute x2, waiting for transfers between devices, shift(): return lax.ppermute(block, axis, route)  3 us
    ppermute x2, waiting for transfers between devices, swap(): lax.ppermute(block, axis, [p for i in pairs for p in ((i, i + 1), (i + 1,...  0.95 us
  transfers between devices with their start and end apart: 4, of which 3 were waited for; matrix products, arithmetic and copies ran while one was open for 0% of the time, Pallas kernels for 8%

profile of v5, /device:TPU:122, one launch (start us, length us, event | category | flops | bytes accessed | tf_op | source)
XLA Modules:
  0.0 24.5 jit_solution(13977702684144783127)
XLA Ops:
  0.6 3.7 %shard_map.59 = (f32[136,384]{1,0:T(8,128)S(1)}, f32[128,256]{1,0:T(8,128)S(1)}, f32[80,384]{1,0:T(8,128)S(1)}, f32[80,384]{1,0:T(8,128)S(1)}) custom-call(s32[4,4096]{1,0:T(4,128)} %boxes_in.1, s32[32,128]{1,0:T(8,128)} %bitcast.3, s32[2,16384]{1,0:T(2,128)} %bins_in.1, s32[128,128]{1,0:T(8,128)} %bitcast.2), custom_call_target="tpu_custom_call" | custom-call | tf_op jit(solution)/shard_map/pallas_call | solution.py:298
  4.3 1.9 %collective-permute-start = (f32[80,384]{1,0:T(8,128)S(1)}, f32[80,384]{1,0:T(8,128)S(1)}, u32[]{:S(2)}, u32[]{:S(2)}) collective-permute-start(f32[80,384]{1,0:T(8,128)S(1)} %get-tuple-element.17), channel_id=1, source_target_pairs={{16,32},{32,16},{48,64},{64,48},{80,96},{96,80},{112,128},{128,112... | collective-permute-start | bytes 368648 | tf_op jit(solution)/shard_map/ppermute | solution.py:288
  6.2 5.1 %collective-permute-start.1 = (f32[80,384]{1,0:T(8,128)S(1)}, f32[80,384]{1,0:T(8,128)S(1)}, u32[]{:S(2)}, u32[]{:S(2)}) collective-permute-start(f32[80,384]{1,0:T(8,128)S(1)} %get-tuple-element.18), channel_id=1, source_target_pairs={{0,16},{16,0},{32,48},{48,32},{64,80},{80,64},{96,112},{112,96},{1... | collective-permute-start | bytes 368648 | tf_op jit(solution)/shard_map/ppermute | solution.py:288
  11.4 0.0 collective-permute-done.odd_in
  11.4 0.9 %collective-permute-done.1.even_in = f32[80,384]{1,0:T(8,128)S(1)} collective-permute-done((f32[80,384]{1,0:T(8,128)S(1)}, f32[80,384]{1,0:T(8,128)S(1)}, u32[]{:S(2)}, u32[]{:S(2)}) %collective-permute-start.1) | collective-permute-done | bytes 122912 | tf_op jit(solution)/shard_map/ppermute | solution.py:288
  12.3 0.2 shard_map.60
  12.5 3.1 %collective-permute-start.2 = (f32[176,128]{1,0:T(8,128)S(1)}, f32[176,128]{1,0:T(8,128)S(1)}, u32[]{:S(2)}, u32[]{:S(2)}) collective-permute-start(f32[176,128]{1,0:T(8,128)S(1)} %get-tuple-element.23), channel_id=1, source_target_pairs={{0,1},{1,2},{2,3},{3,4},{4,5},{5,6},{6,7},{7,8},{8,9},{9,10},{10,1... | collective-permute-start | bytes 270344 | tf_op jit(solution)/shard_map/ppermute | solution.py:294
  15.6 2.8 %collective-permute-start.3 = (f32[32,128]{1,0:T(8,128)S(1)}, f32[32,128]{1,0:T(8,128)S(1)}, u32[]{:S(2)}, u32[]{:S(2)}) collective-permute-start(f32[32,128]{1,0:T(8,128)S(1)} %get-tuple-element.27), channel_id=1, source_target_pairs={{1,0},{2,1},{3,2},{4,3},{5,4},{6,5},{7,6},{8,7},{9,8},{10,9},{11,1... | collective-permute-start | bytes 49160 | tf_op jit(solution)/shard_map/ppermute | solution.py:294
  18.4 0.6 %shard_map.61 = (f32[144,256]{1,0:T(8,128)S(1)}, f32[144,256]{1,0:T(8,128)S(1)}, f32[8,256]{1,0:T(8,128)S(1)}) custom-call(f32[144,384]{1,0:T(8,128)S(1)} %get-tuple-element.19.d_in, f32[144,256]{1,0:T(8,128)S(1)} %get-tuple-element.20.a_in), custom_call_target="tpu_custom_call" | custom-call | tf_op jit(solution)/shard_map/pallas_call | solution.py:298
  19.0 0.3 %collective-permute-done.2.left = f32[176,128]{1,0:T(8,128)S(1)} collective-permute-done((f32[176,128]{1,0:T(8,128)S(1)}, f32[176,128]{1,0:T(8,128)S(1)}, u32[]{:S(2)}, u32[]{:S(2)}) %collective-permute-start.2) | collective-permute-done | bytes 90144 | tf_op jit(solution)/shard_map/ppermute | solution.py:294
  19.3 1.3 %shard_map.62 = (f32[128,256]{1,0:T(8,128)}, f32[2,144,128]{2,1,0:T(8,128)S(1)}) custom-call(f32[144,384]{1,0:T(8,128)S(1)} %get-tuple-element.19.d_in, f32[144,256]{1,0:T(8,128)S(1)} %get-tuple-element.20.a_in, f32[144,256]{1,0:T(8,128)S(1)} %get-tuple-element.21.spread, f32[144,256]{1,0:T(8,128)S(1)} %get-tuple-element.22.mask, ...), custom_call_target="tpu_custom_call" | custom-call | tf_op jit(solution)/shard_map/pallas_call | solution.py:298
  20.6 2.8 %collective-permute-done.3.right = f32[32,128]{1,0:T(8,128)S(1)} collective-permute-done((f32[32,128]{1,0:T(8,128)S(1)}, f32[32,128]{1,0:T(8,128)S(1)}, u32[]{:S(2)}, u32[]{:S(2)}) %collective-permute-start.3) | collective-permute-done | bytes 16416 | tf_op jit(solution)/shard_map/ppermute | solution.py:294
  23.3 1.2 %shard_map.63 = f32[128,256]{1,0:T(8,128)} custom-call(f32[2,144,128]{2,1,0:T(8,128)S(1)} %get-tuple-element.25.spread, f32[8,256]{1,0:T(8,128)S(1)} %get-tuple-element.26.over, f32[32,128]{1,0:T(8,128)S(1)} %collective-permute-done.3.right), custom_call_target="tpu_custom_call" | custom-call | tf_op jit(solution)/shard_map/pallas_call | solution.py:298
Async XLA Ops:
  4.3 7.1 %collective-permute-start = (f32[80,384]{1,0:T(8,128)S(1)}, f32[80,384]{1,0:T(8,128)S(1)}, u32[]{:S(2)}, u32[]{:S(2)}) collective-permute-start(f32[80,384]{1,0:T(8,128)S(1)} %get-tuple-element.17), channel_id=1, source_target_pairs={{16,32},{32,16},{48,64},{64,48},{80,96},{96,80},{112,128},{128,112... | collective-permute-start | bytes 368648 | tf_op jit(solution)/shard_map/ppermute | solution.py:288
  6.2 6.1 %collective-permute-start.1 = (f32[80,384]{1,0:T(8,128)S(1)}, f32[80,384]{1,0:T(8,128)S(1)}, u32[]{:S(2)}, u32[]{:S(2)}) collective-permute-start(f32[80,384]{1,0:T(8,128)S(1)} %get-tuple-element.18), channel_id=1, source_target_pairs={{0,16},{16,0},{32,48},{48,32},{64,80},{80,64},{96,112},{112,96},{1... | collective-permute-start | bytes 368648 | tf_op jit(solution)/shard_map/ppermute | solution.py:288
  12.5 6.8 %collective-permute-start.2 = (f32[176,128]{1,0:T(8,128)S(1)}, f32[176,128]{1,0:T(8,128)S(1)}, u32[]{:S(2)}, u32[]{:S(2)}) collective-permute-start(f32[176,128]{1,0:T(8,128)S(1)} %get-tuple-element.23), channel_id=1, source_target_pairs={{0,1},{1,2},{2,3},{3,4},{4,5},{5,6},{6,7},{7,8},{8,9},{9,10},{10,1... | collective-permute-start | bytes 270344 | tf_op jit(solution)/shard_map/ppermute | solution.py:294
  15.6 7.7 %collective-permute-start.3 = (f32[32,128]{1,0:T(8,128)S(1)}, f32[32,128]{1,0:T(8,128)S(1)}, u32[]{:S(2)}, u32[]{:S(2)}) collective-permute-start(f32[32,128]{1,0:T(8,128)S(1)} %get-tuple-element.27), channel_id=1, source_target_pairs={{1,0},{2,1},{3,2},{4,3},{5,4},{6,5},{7,6},{8,7},{9,8},{10,9},{11,1... | collective-permute-start | bytes 49160 | tf_op jit(solution)/shard_map/ppermute | solution.py:294

commit v6 on v5

--- a/solution.py
+++ b/solution.py
@@ -11,7 +11,7 @@
 PART = (BR + 16) // 8
 TALL = 192
 WIDE = 384
-NET_BLOCK = 4096
+NET_BLOCK = 2048
 CELL_BLOCK = 8192
 FACTORS = 24
 F32 = jnp.float32
@@ -71,22 +71,29 @@
     boxes_in, pins_in, bins_in, area_in, d_out, a_out, even_out, odd_out,
     boxes, pins, bins, area, row_factor, col_factor, sems,
 ):
+    half = boxes.shape[1] // 2
     copies = [
         pltpu.make_async_copy(source, target, sems.at[i])
         for i, (source, target) in enumerate(
-            ((boxes_in, boxes), (pins_in, pins), (bins_in, bins), (area_in, area))
+            (
+                (boxes_in.at[:, :half], boxes.at[:, :half]),
+                (boxes_in.at[:, half:], boxes.at[:, half:]),
+                (pins_in, pins),
+                (bins_in, bins),
+                (area_in, area),
+            )
         )
     ]
     for copy in copies:
         copy.start()
-    copies[0].wait()
-    copies[1].wait()
+    for copy in copies[:3]:
+        copy.wait()
     split_weights(boxes, pins, row_factor, col_factor)
     n = NET_BLOCK
     zero = jnp.zeros((), BF16)
 
     def add_nets(i, demand):
-        k = i * n
+        k = pl.multiple_of(i * n, n)
         box = boxes[:, pl.ds(k, n)]
         y0, y1, x0, x1 = (box[i : i + 1] for i in range(4))
         top = y0 & (BR - 1)
@@ -103,11 +110,10 @@
         right = jnp.where(inside, repeated(lane_row(col_factor, k, n), 16, BF16), zero)
         return demand + nt_dot(right.reshape(WIDE, n), down.reshape(TALL, n))
 
-    demand = add_nets(0, jnp.zeros((WIDE, TALL), F32))
-    copies[2].wait()
-    copies[3].wait()
+    for copy in copies[3:]:
+        copy.wait()
     m = CELL_BLOCK
-    zero = jnp.zeros((), FP8)
+    none = jnp.zeros((), FP8)
     one = jnp.ones((), FP8)
 
     def add_cells(i, total):
@@ -117,7 +123,7 @@
         rows = ruler(BR, 32, 0, m, jnp.int8) == repeated(where[0:1] & (BR - 1), 32, jnp.int8)
         down = jnp.concatenate(
             [
-                jnp.where(rows, repeated(part, 32, FP8), zero).reshape(BR, m)
+                jnp.where(rows, repeated(part, 32, FP8), none).reshape(BR, m)
                 for part in (size >> 3, size & 7)
             ],
             axis=0,
@@ -125,10 +131,15 @@
         cols = ruler(BC, 32, 128, m, jnp.int8) == repeated(
             (where[1:2] & (BC - 1)) - 128, 32, jnp.int8
         )
-        right = jnp.where(cols, one, zero).reshape(BC, m)
+        right = jnp.where(cols, one, none).reshape(BC, m)
         return total + nt_dot(down, right)
 
-    total = lax.fori_loop(0, bins.shape[1] // m, add_cells, jnp.zeros((2 * BR, BC), F32))
+    demand, total = lax.fori_loop(
+        0,
+        boxes.shape[1] // n,
+        lambda i, sums: (add_nets(i, sums[0]), add_cells(i, sums[1])),
+        (jnp.zeros((WIDE, TALL), F32), jnp.zeros((2 * BR, BC), F32)),
+    )
     demand = demand.T
     total = total[:BR] * 0.5 + total[BR:] * (1.0 / 16.0)
     d_out[...] = demand[: BR + 8]
@@ -317,7 +328,7 @@
         space=HBM,
         scratch=[pltpu.VMEM(a.shape, a.dtype) for a in inputs]
         + [pltpu.VMEM(pins.shape, F32)] * 2
-        + [pltpu.SemaphoreType.DMA((4,))],
+        + [pltpu.SemaphoreType.DMA((5,))],
     )
     odd = swap(odd, "row", 1)
     even = swap(even, "row", 0)

time: 24.7 us -> 24.6 us (level)
  the two profiles are of different devices: /device:TPU:122 before, /device:TPU:250 now
where the time goes in v6:
time: 24.6 us; the launch traced here: 24.4 us
  starting transfers between devices  12.9 us (52%)
  Pallas kernels  6.88 us (28%)
  waiting for transfers between devices  3.95 us (16%)
  between operations  0.7 us (3%)
    ppermute x2, starting transfers between devices, swap(): lax.ppermute(block, axis, [p for i in pairs for p in ((i, i + 1), (i + 1,...  7.06 us
    pallas_call x5, Pallas kernels, call(): pl.pallas_call(kernel, out_shape=[jax.ShapeDtypeStruct(s, F32) for s in s...  6.88 us
    ppermute x2, starting transfers between devices, shift(): return lax.ppermute(block, axis, route)  5.86 us
    ppermute x2, waiting for transfers between devices, shift(): return lax.ppermute(block, axis, route)  3 us
    ppermute x2, waiting for transfers between devices, swap(): lax.ppermute(block, axis, [p for i in pairs for p in ((i, i + 1), (i + 1,...  0.95 us
  transfers between devices with their start and end apart: 4, of which 3 were waited for; matrix products, arithmetic and copies ran while one was open for 0% of the time, Pallas kernels for 8%

profile of v6, /device:TPU:250, one launch (start us, length us, event | category | flops | bytes accessed | tf_op | source)
XLA Modules:
  0.0 24.4 jit_solution(567120635602277406)
XLA Ops:
  0.6 3.6 %shard_map.59 = (f32[136,384]{1,0:T(8,128)S(1)}, f32[128,256]{1,0:T(8,128)S(1)}, f32[80,384]{1,0:T(8,128)S(1)}, f32[80,384]{1,0:T(8,128)S(1)}) custom-call(s32[4,4096]{1,0:T(4,128)} %boxes_in.1, s32[32,128]{1,0:T(8,128)} %bitcast.3, s32[2,16384]{1,0:T(2,128)} %bins_in.1, s32[128,128]{1,0:T(8,128)} %bitcast.2), custom_call_target="tpu_custom_call" | custom-call | tf_op jit(solution)/shard_map/pallas_call | solution.py:309
  4.2 1.9 %collective-permute-start = (f32[80,384]{1,0:T(8,128)S(1)}, f32[80,384]{1,0:T(8,128)S(1)}, u32[]{:S(2)}, u32[]{:S(2)}) collective-permute-start(f32[80,384]{1,0:T(8,128)S(1)} %get-tuple-element.17), channel_id=1, source_target_pairs={{16,32},{32,16},{48,64},{64,48},{80,96},{96,80},{112,128},{128,112... | collective-permute-start | bytes 368648 | tf_op jit(solution)/shard_map/ppermute | solution.py:299
  6.2 5.1 %collective-permute-start.1 = (f32[80,384]{1,0:T(8,128)S(1)}, f32[80,384]{1,0:T(8,128)S(1)}, u32[]{:S(2)}, u32[]{:S(2)}) collective-permute-start(f32[80,384]{1,0:T(8,128)S(1)} %get-tuple-element.18), channel_id=1, source_target_pairs={{0,16},{16,0},{32,48},{48,32},{64,80},{80,64},{96,112},{112,96},{1... | collective-permute-start | bytes 368648 | tf_op jit(solution)/shard_map/ppermute | solution.py:299
  11.3 0.0 collective-permute-done.odd_in
  11.3 0.9 %collective-permute-done.1.even_in = f32[80,384]{1,0:T(8,128)S(1)} collective-permute-done((f32[80,384]{1,0:T(8,128)S(1)}, f32[80,384]{1,0:T(8,128)S(1)}, u32[]{:S(2)}, u32[]{:S(2)}) %collective-permute-start.1) | collective-permute-done | bytes 122912 | tf_op jit(solution)/shard_map/ppermute | solution.py:299
  12.3 0.2 shard_map.60
  12.4 3.1 %collective-permute-start.2 = (f32[176,128]{1,0:T(8,128)S(1)}, f32[176,128]{1,0:T(8,128)S(1)}, u32[]{:S(2)}, u32[]{:S(2)}) collective-permute-start(f32[176,128]{1,0:T(8,128)S(1)} %get-tuple-element.23), channel_id=1, source_target_pairs={{0,1},{1,2},{2,3},{3,4},{4,5},{5,6},{6,7},{7,8},{8,9},{9,10},{10,1... | collective-permute-start | bytes 270344 | tf_op jit(solution)/shard_map/ppermute | solution.py:305
  15.5 2.8 %collective-permute-start.3 = (f32[32,128]{1,0:T(8,128)S(1)}, f32[32,128]{1,0:T(8,128)S(1)}, u32[]{:S(2)}, u32[]{:S(2)}) collective-permute-start(f32[32,128]{1,0:T(8,128)S(1)} %get-tuple-element.27), channel_id=1, source_target_pairs={{1,0},{2,1},{3,2},{4,3},{5,4},{6,5},{7,6},{8,7},{9,8},{10,9},{11,1... | collective-permute-start | bytes 49160 | tf_op jit(solution)/shard_map/ppermute | solution.py:305
  18.3 0.6 %shard_map.61 = (f32[144,256]{1,0:T(8,128)S(1)}, f32[144,256]{1,0:T(8,128)S(1)}, f32[8,256]{1,0:T(8,128)S(1)}) custom-call(f32[144,384]{1,0:T(8,128)S(1)} %get-tuple-element.19.d_in, f32[144,256]{1,0:T(8,128)S(1)} %get-tuple-element.20.a_in), custom_call_target="tpu_custom_call" | custom-call | tf_op jit(solution)/shard_map/pallas_call | solution.py:309
  19.0 0.3 %collective-permute-done.2.left = f32[176,128]{1,0:T(8,128)S(1)} collective-permute-done((f32[176,128]{1,0:T(8,128)S(1)}, f32[176,128]{1,0:T(8,128)S(1)}, u32[]{:S(2)}, u32[]{:S(2)}) %collective-permute-start.2) | collective-permute-done | bytes 90144 | tf_op jit(solution)/shard_map/ppermute | solution.py:305
  19.2 1.3 %shard_map.62 = (f32[128,256]{1,0:T(8,128)}, f32[2,144,128]{2,1,0:T(8,128)S(1)}) custom-call(f32[144,384]{1,0:T(8,128)S(1)} %get-tuple-element.19.d_in, f32[144,256]{1,0:T(8,128)S(1)} %get-tuple-element.20.a_in, f32[144,256]{1,0:T(8,128)S(1)} %get-tuple-element.21.spread, f32[144,256]{1,0:T(8,128)S(1)} %get-tuple-element.22.mask, ...), custom_call_target="tpu_custom_call" | custom-call | tf_op jit(solution)/shard_map/pallas_call | solution.py:309
  20.5 2.8 %collective-permute-done.3.right = f32[32,128]{1,0:T(8,128)S(1)} collective-permute-done((f32[32,128]{1,0:T(8,128)S(1)}, f32[32,128]{1,0:T(8,128)S(1)}, u32[]{:S(2)}, u32[]{:S(2)}) %collective-permute-start.3) | collective-permute-done | bytes 16416 | tf_op jit(solution)/shard_map/ppermute | solution.py:305
  23.3 1.2 %shard_map.63 = f32[128,256]{1,0:T(8,128)} custom-call(f32[2,144,128]{2,1,0:T(8,128)S(1)} %get-tuple-element.25.spread, f32[8,256]{1,0:T(8,128)S(1)} %get-tuple-element.26.over, f32[32,128]{1,0:T(8,128)S(1)} %collective-permute-done.3.right), custom_call_target="tpu_custom_call" | custom-call | tf_op jit(solution)/shard_map/pallas_call | solution.py:309
Async XLA Ops:
  4.2 7.1 %collective-permute-start = (f32[80,384]{1,0:T(8,128)S(1)}, f32[80,384]{1,0:T(8,128)S(1)}, u32[]{:S(2)}, u32[]{:S(2)}) collective-permute-start(f32[80,384]{1,0:T(8,128)S(1)} %get-tuple-element.17), channel_id=1, source_target_pairs={{16,32},{32,16},{48,64},{64,48},{80,96},{96,80},{112,128},{128,112... | collective-permute-start | bytes 368648 | tf_op jit(solution)/shard_map/ppermute | solution.py:299
  6.2 6.1 %collective-permute-start.1 = (f32[80,384]{1,0:T(8,128)S(1)}, f32[80,384]{1,0:T(8,128)S(1)}, u32[]{:S(2)}, u32[]{:S(2)}) collective-permute-start(f32[80,384]{1,0:T(8,128)S(1)} %get-tuple-element.18), channel_id=1, source_target_pairs={{0,16},{16,0},{32,48},{48,32},{64,80},{80,64},{96,112},{112,96},{1... | collective-permute-start | bytes 368648 | tf_op jit(solution)/shard_map/ppermute | solution.py:299
  12.4 6.8 %collective-permute-start.2 = (f32[176,128]{1,0:T(8,128)S(1)}, f32[176,128]{1,0:T(8,128)S(1)}, u32[]{:S(2)}, u32[]{:S(2)}) collective-permute-start(f32[176,128]{1,0:T(8,128)S(1)} %get-tuple-element.23), channel_id=1, source_target_pairs={{0,1},{1,2},{2,3},{3,4},{4,5},{5,6},{6,7},{7,8},{8,9},{9,10},{10,1... | collective-permute-start | bytes 270344 | tf_op jit(solution)/shard_map/ppermute | solution.py:305
  15.5 7.7 %collective-permute-start.3 = (f32[32,128]{1,0:T(8,128)S(1)}, f32[32,128]{1,0:T(8,128)S(1)}, u32[]{:S(2)}, u32[]{:S(2)}) collective-permute-start(f32[32,128]{1,0:T(8,128)S(1)} %get-tuple-element.27), channel_id=1, source_target_pairs={{1,0},{2,1},{3,2},{4,3},{5,4},{6,5},{7,6},{8,7},{9,8},{10,9},{11,1... | collective-permute-start | bytes 49160 | tf_op jit(solution)/shard_map/ppermute | solution.py:305

commit v7 on v6

--- a/solution.py
+++ b/solution.py
@@ -134,11 +134,11 @@
         right = jnp.where(cols, one, none).reshape(BC, m)
         return total + nt_dot(down, right)
 
-    demand, total = lax.fori_loop(
+    total, demand = lax.fori_loop(
         0,
         boxes.shape[1] // n,
-        lambda i, sums: (add_nets(i, sums[0]), add_cells(i, sums[1])),
-        (jnp.zeros((WIDE, TALL), F32), jnp.zeros((2 * BR, BC), F32)),
+        lambda i, sums: (add_cells(i, sums[0]), add_nets(i, sums[1])),
+        (jnp.zeros((2 * BR, BC), F32), jnp.zeros((WIDE, TALL), F32)),
     )
     demand = demand.T
     total = total[:BR] * 0.5 + total[BR:] * (1.0 / 16.0)

time: 24.6 us -> 24.6 us (level)
  the two profiles are of different devices: /device:TPU:250 before, /device:TPU:122 now
where the time goes in v7:
time: 24.6 us; the launch traced here: 24.4 us
  starting transfers between devices  12.9 us (52%)
  Pallas kernels  6.86 us (28%)
  waiting for transfers between devices  3.95 us (16%)
  between operations  0.7 us (3%)
    ppermute x2, starting transfers between devices, swap(): lax.ppermute(block, axis, [p for i in pairs for p in ((i, i + 1), (i + 1,...  7.06 us
    pallas_call x5, Pallas kernels, call(): pl.pallas_call(kernel, out_shape=[jax.ShapeDtypeStruct(s, F32) for s in s...  6.86 us
    ppermute x2, starting transfers between devices, shift(): return lax.ppermute(block, axis, route)  5.86 us
    ppermute x2, waiting for transfers between devices, shift(): return lax.ppermute(block, axis, route)  3 us
    ppermute x2, waiting for transfers between devices, swap(): lax.ppermute(block, axis, [p for i in pairs for p in ((i, i + 1), (i + 1,...  0.95 us
  transfers between devices with their start and end apart: 4, of which 3 were waited for; matrix products, arithmetic and copies ran while one was open for 0% of the time, Pallas kernels for 8%

profile of v7, /device:TPU:122, one launch (start us, length us, event | category | flops | bytes accessed | tf_op | source)
XLA Modules:
  0.0 24.4 jit_solution(13210973921536956098)
XLA Ops:
  0.6 3.6 %shard_map.59 = (f32[136,384]{1,0:T(8,128)S(1)}, f32[128,256]{1,0:T(8,128)S(1)}, f32[80,384]{1,0:T(8,128)S(1)}, f32[80,384]{1,0:T(8,128)S(1)}) custom-call(s32[4,4096]{1,0:T(4,128)} %boxes_in.1, s32[32,128]{1,0:T(8,128)} %bitcast.3, s32[2,16384]{1,0:T(2,128)} %bins_in.1, s32[128,128]{1,0:T(8,128)} %bitcast.2), custom_call_target="tpu_custom_call" | custom-call | tf_op jit(solution)/shard_map/pallas_call | solution.py:309
  4.2 1.9 %collective-permute-start = (f32[80,384]{1,0:T(8,128)S(1)}, f32[80,384]{1,0:T(8,128)S(1)}, u32[]{:S(2)}, u32[]{:S(2)}) collective-permute-start(f32[80,384]{1,0:T(8,128)S(1)} %get-tuple-element.17), channel_id=1, source_target_pairs={{16,32},{32,16},{48,64},{64,48},{80,96},{96,80},{112,128},{128,112... | collective-permute-start | bytes 368648 | tf_op jit(solution)/shard_map/ppermute | solution.py:299
  6.1 5.1 %collective-permute-start.1 = (f32[80,384]{1,0:T(8,128)S(1)}, f32[80,384]{1,0:T(8,128)S(1)}, u32[]{:S(2)}, u32[]{:S(2)}) collective-permute-start(f32[80,384]{1,0:T(8,128)S(1)} %get-tuple-element.18), channel_id=1, source_target_pairs={{0,16},{16,0},{32,48},{48,32},{64,80},{80,64},{96,112},{112,96},{1... | collective-permute-start | bytes 368648 | tf_op jit(solution)/shard_map/ppermute | solution.py:299
  11.3 0.0 collective-permute-done.odd_in
  11.3 0.9 %collective-permute-done.1.even_in = f32[80,384]{1,0:T(8,128)S(1)} collective-permute-done((f32[80,384]{1,0:T(8,128)S(1)}, f32[80,384]{1,0:T(8,128)S(1)}, u32[]{:S(2)}, u32[]{:S(2)}) %collective-permute-start.1) | collective-permute-done | bytes 122912 | tf_op jit(solution)/shard_map/ppermute | solution.py:299
  12.2 0.2 shard_map.60
  12.4 3.1 %collective-permute-start.2 = (f32[176,128]{1,0:T(8,128)S(1)}, f32[176,128]{1,0:T(8,128)S(1)}, u32[]{:S(2)}, u32[]{:S(2)}) collective-permute-start(f32[176,128]{1,0:T(8,128)S(1)} %get-tuple-element.23), channel_id=1, source_target_pairs={{0,1},{1,2},{2,3},{3,4},{4,5},{5,6},{6,7},{7,8},{8,9},{9,10},{10,1... | collective-permute-start | bytes 270344 | tf_op jit(solution)/shard_map/ppermute | solution.py:305
  15.5 2.8 %collective-permute-start.3 = (f32[32,128]{1,0:T(8,128)S(1)}, f32[32,128]{1,0:T(8,128)S(1)}, u32[]{:S(2)}, u32[]{:S(2)}) collective-permute-start(f32[32,128]{1,0:T(8,128)S(1)} %get-tuple-element.27), channel_id=1, source_target_pairs={{1,0},{2,1},{3,2},{4,3},{5,4},{6,5},{7,6},{8,7},{9,8},{10,9},{11,1... | collective-permute-start | bytes 49160 | tf_op jit(solution)/shard_map/ppermute | solution.py:305
  18.3 0.6 %shard_map.61 = (f32[144,256]{1,0:T(8,128)S(1)}, f32[144,256]{1,0:T(8,128)S(1)}, f32[8,256]{1,0:T(8,128)S(1)}) custom-call(f32[144,384]{1,0:T(8,128)S(1)} %get-tuple-element.19.d_in, f32[144,256]{1,0:T(8,128)S(1)} %get-tuple-element.20.a_in), custom_call_target="tpu_custom_call" | custom-call | tf_op jit(solution)/shard_map/pallas_call | solution.py:309
  19.0 0.3 %collective-permute-done.2.left = f32[176,128]{1,0:T(8,128)S(1)} collective-permute-done((f32[176,128]{1,0:T(8,128)S(1)}, f32[176,128]{1,0:T(8,128)S(1)}, u32[]{:S(2)}, u32[]{:S(2)}) %collective-permute-start.2) | collective-permute-done | bytes 90144 | tf_op jit(solution)/shard_map/ppermute | solution.py:305
  19.2 1.3 %shard_map.62 = (f32[128,256]{1,0:T(8,128)}, f32[2,144,128]{2,1,0:T(8,128)S(1)}) custom-call(f32[144,384]{1,0:T(8,128)S(1)} %get-tuple-element.19.d_in, f32[144,256]{1,0:T(8,128)S(1)} %get-tuple-element.20.a_in, f32[144,256]{1,0:T(8,128)S(1)} %get-tuple-element.21.spread, f32[144,256]{1,0:T(8,128)S(1)} %get-tuple-element.22.mask, ...), custom_call_target="tpu_custom_call" | custom-call | tf_op jit(solution)/shard_map/pallas_call | solution.py:309
  20.5 2.8 %collective-permute-done.3.right = f32[32,128]{1,0:T(8,128)S(1)} collective-permute-done((f32[32,128]{1,0:T(8,128)S(1)}, f32[32,128]{1,0:T(8,128)S(1)}, u32[]{:S(2)}, u32[]{:S(2)}) %collective-permute-start.3) | collective-permute-done | bytes 16416 | tf_op jit(solution)/shard_map/ppermute | solution.py:305
  23.2 1.2 %shard_map.63 = f32[128,256]{1,0:T(8,128)} custom-call(f32[2,144,128]{2,1,0:T(8,128)S(1)} %get-tuple-element.25.spread, f32[8,256]{1,0:T(8,128)S(1)} %get-tuple-element.26.over, f32[32,128]{1,0:T(8,128)S(1)} %collective-permute-done.3.right), custom_call_target="tpu_custom_call" | custom-call | tf_op jit(solution)/shard_map/pallas_call | solution.py:309
Async XLA Ops:
  4.2 7.1 %collective-permute-start = (f32[80,384]{1,0:T(8,128)S(1)}, f32[80,384]{1,0:T(8,128)S(1)}, u32[]{:S(2)}, u32[]{:S(2)}) collective-permute-start(f32[80,384]{1,0:T(8,128)S(1)} %get-tuple-element.17), channel_id=1, source_target_pairs={{16,32},{32,16},{48,64},{64,48},{80,96},{96,80},{112,128},{128,112... | collective-permute-start | bytes 368648 | tf_op jit(solution)/shard_map/ppermute | solution.py:299
  6.1 6.1 %collective-permute-start.1 = (f32[80,384]{1,0:T(8,128)S(1)}, f32[80,384]{1,0:T(8,128)S(1)}, u32[]{:S(2)}, u32[]{:S(2)}) collective-permute-start(f32[80,384]{1,0:T(8,128)S(1)} %get-tuple-element.18), channel_id=1, source_target_pairs={{0,16},{16,0},{32,48},{48,32},{64,80},{80,64},{96,112},{112,96},{1... | collective-permute-start | bytes 368648 | tf_op jit(solution)/shard_map/ppermute | solution.py:299
  12.4 6.8 %collective-permute-start.2 = (f32[176,128]{1,0:T(8,128)S(1)}, f32[176,128]{1,0:T(8,128)S(1)}, u32[]{:S(2)}, u32[]{:S(2)}) collective-permute-start(f32[176,128]{1,0:T(8,128)S(1)} %get-tuple-element.23), channel_id=1, source_target_pairs={{0,1},{1,2},{2,3},{3,4},{4,5},{5,6},{6,7},{7,8},{8,9},{9,10},{10,1... | collective-permute-start | bytes 270344 | tf_op jit(solution)/shard_map/ppermute | solution.py:305
  15.5 7.7 %collective-permute-start.3 = (f32[32,128]{1,0:T(8,128)S(1)}, f32[32,128]{1,0:T(8,128)S(1)}, u32[]{:S(2)}, u32[]{:S(2)}) collective-permute-start(f32[32,128]{1,0:T(8,128)S(1)} %get-tuple-element.27), channel_id=1, source_target_pairs={{1,0},{2,1},{3,2},{4,3},{5,4},{6,5},{7,6},{8,7},{9,8},{10,9},{11,1... | collective-permute-start | bytes 49160 | tf_op jit(solution)/shard_map/ppermute | solution.py:305
